TPU v7x, 32 devices: a whole 2x2x4 slice. The times are simulated.
32 devices in a mesh: dp: 16 (over z, y, core), seq: 2 (over x).
Axes of the slice: x: 2, y: 2, z: 4, core: 2. Of those that a mesh axis runs over, the one named last changes fastest.
Arguments:
- tokens: bfloat16 [16, 322, 1152], P('dp', 'seq'), may hold values from -6 to 6
- skip_feats: bfloat16 [16, 322, 1152], P('dp', None, 'seq'), may hold values from -6 to 6
- lengths: int32 [16], P('dp'), may hold values from 194 to 322, as said below
- cotangent: bfloat16 [16, 322, 1152], P('dp', 'seq'), may hold values from -6 to 6
- skip_weight: bfloat16 [2304, 1152], replicated, may hold values from -0.125 to 0.125
- skip_bias: bfloat16 [1152], replicated, may hold values from -2 to 2
- norm1_gain: bfloat16 [1152], replicated, may hold values from 0.099609375 to 1.8984375
- norm1_bias: bfloat16 [1152], replicated, may hold values from -2 to 2
- qkv_weight: bfloat16 [1152, 3456], replicated, may hold values from -0.1875 to 0.1875
- proj_weight: bfloat16 [1152, 1152], replicated, may hold values from -1.5 to 1.5
- proj_bias: bfloat16 [1152], replicated, may hold values from -2 to 2
- norm2_gain: bfloat16 [1152], replicated, may hold values from 0.099609375 to 1.8984375
- norm2_bias: bfloat16 [1152], replicated, may hold values from -2 to 2
- fc1_weight: bfloat16 [1152, 4608], replicated, may hold values from -0.1875 to 0.1875
- fc1_bias: bfloat16 [4608], replicated, may hold values from -2 to 2
- fc2_weight: bfloat16 [4608, 1152], replicated, may hold values from -0.09375 to 0.09375
- fc2_bias: bfloat16 [1152], replicated, may hold values from -2 to 2
Outputs:
- block_out: bfloat16 [16, 322, 1152], P('dp', 'seq')
- tokens_grad: bfloat16 [16, 322, 1152], P('dp', 'seq')
- skip_grad: bfloat16 [16, 322, 1152], P('dp', None, 'seq')
- skip_weight_grad: float32 [2304, 1152], P(('dp', 'seq'))
- skip_bias_grad: float32 [1152], P(('dp', 'seq'))
- norm1_gain_grad: float32 [1152], P(('dp', 'seq'))
- norm1_bias_grad: float32 [1152], P(('dp', 'seq'))
- qkv_weight_grad: float32 [1152, 3456], P(('dp', 'seq'))
- proj_weight_grad: float32 [1152, 1152], P(('dp', 'seq'))
- proj_bias_grad: float32 [1152], P(('dp', 'seq'))
- norm2_gain_grad: float32 [1152], P(('dp', 'seq'))
- norm2_bias_grad: float32 [1152], P(('dp', 'seq'))
- fc1_weight_grad: float32 [1152, 4608], P(('dp', 'seq'))
- fc1_bias_grad: float32 [4608], P(('dp', 'seq'))
- fc2_weight_grad: float32 [4608, 1152], P(('dp', 'seq'))
- fc2_bias_grad: float32 [1152], P(('dp', 'seq'))
Inputs may be any that keep to these rules, and one draw needn't show every extreme that they name: `lengths`: slots of an item at or beyond its length are padding. Some item uses all 322 slots in every draw, and some item uses the fewest.
All inputs are finite; a program needn't handle non-finite values.
Results may differ from a plain program's by a relative error of at most 0.015.
Values may be sent and summed in bfloat16 or wider, within the bound.
A program may use at most 192 MiB of HBM per device.

v0:
```python
import jax
import jax.numpy as jnp
from jax import lax
from jax.sharding import PartitionSpec as P

HEADS = 16
HEAD_DIM = 72


NORM_EPS = 1e-05
MASKED = -1e30


def layer_norm(v, gain, bias):
    row_mean = jnp.mean(v, axis=-1, keepdims=True)
    centred = v - row_mean
    variance = jnp.mean(centred * centred, axis=-1, keepdims=True)
    return centred * lax.rsqrt(variance + NORM_EPS) * gain + bias


def gelu_exact(v):
    return jax.nn.gelu(v, approximate=False)


def matmul(form, left, right):
    return jnp.einsum(form, left, right, preferred_element_type=jnp.float32)


def own_features(left, seq_pos, dp_count, seq_count):
    item_count, slot_count, feat_total = left.shape
    block_width = feat_total // (dp_count * seq_count)
    blocks = left.reshape(item_count, slot_count, dp_count, seq_count, block_width)
    picked = lax.dynamic_index_in_dim(blocks, seq_pos, 3, keepdims=False)
    return picked.reshape(item_count, slot_count, dp_count * block_width)


def weight_rows(left, right, seq_pos, dp_count, seq_count):
    return matmul("isc,isd->cd", own_features(left, seq_pos, dp_count, seq_count), right)


def shards(
    tokens,
    skip_feats,
    lengths,
    cotangent,
    skip_weight,
    skip_bias,
    norm1_gain,
    norm1_bias,
    qkv_weight,
    proj_weight,
    proj_bias,
    norm2_gain,
    norm2_bias,
    fc1_weight,
    fc1_bias,
    fc2_weight,
    fc2_bias,
):
    f32 = jnp.float32
    b16 = jnp.bfloat16
    item_count, half, width = tokens.shape
    seq_count = lax.axis_size("seq")
    dp_count = lax.axis_size("dp")
    seq_pos = lax.axis_index("seq")
    slot_count = half * seq_count
    scale = HEAD_DIM ** (-0.5)
    offset = seq_pos * half
    key_valid = jnp.arange(slot_count, dtype=jnp.int32)[None, :] < lengths[:, None]
    own_slots = offset + jnp.arange(half, dtype=jnp.int32)
    row_valid = (own_slots[None, :] < lengths[:, None]).astype(f32)[..., None]
    gain_one = norm1_gain.astype(f32)
    shift_one = norm1_bias.astype(f32)
    gain_two = norm2_gain.astype(f32)
    shift_two = norm2_bias.astype(f32)
    skip_rows = lax.all_to_all(skip_feats, "seq", split_axis=1, concat_axis=2, tiled=True)
    joined = jnp.concatenate([tokens, skip_rows], axis=-1)
    base_sum = matmul("isc,cd->isd", joined, skip_weight) + skip_bias.astype(f32)
    normed_f, norm_pull_one = jax.vjp(layer_norm, base_sum, gain_one, shift_one)
    normed = normed_f.astype(b16)
    packed = matmul("isd,de->ise", normed, qkv_weight).astype(b16)
    query = packed[..., :width]
    key_rows = packed[..., width : 2 * width]
    value_rows = packed[..., 2 * width :]
    key_all, value_all = (
        lax.all_gather(key_rows, "seq", axis=1, tiled=True),
        lax.all_gather(value_rows, "seq", axis=1, tiled=True),
    )
    query_four = query.reshape(item_count, half, HEADS, HEAD_DIM)
    key_four = key_all.reshape(item_count, slot_count, HEADS, HEAD_DIM)
    value_four = value_all.reshape(item_count, slot_count, HEADS, HEAD_DIM)
    raw_scores = matmul("iqhd,ikhd->ihqk", query_four, key_four)
    scores = jnp.where(key_valid[:, None, None, :], raw_scores * scale, MASKED)
    attn_probs = jax.nn.softmax(scores, axis=-1)
    probs_low = attn_probs.astype(b16)
    head_out = (
        matmul("ihqk,ikhd->iqhd", probs_low, value_four)
        .reshape(item_count, half, width)
        .astype(b16)
    )
    middle = base_sum + matmul("isd,de->ise", head_out, proj_weight) + proj_bias.astype(f32)
    normed_two_f, norm_pull_two = jax.vjp(layer_norm, middle, gain_two, shift_two)
    normed_two = normed_two_f.astype(b16)
    active = matmul("isd,df->isf", normed_two, fc1_weight) + fc1_bias.astype(f32)
    hidden_f, gelu_pull = jax.vjp(gelu_exact, active)
    hidden = hidden_f.astype(b16)
    result = middle + matmul("isf,fd->isd", hidden, fc2_weight) + fc2_bias.astype(f32)
    block_out = (result * row_valid).astype(b16)
    d_final = cotangent.astype(f32) * row_valid
    d_final_low = d_final.astype(b16)
    fc2_bias_grad = jnp.sum(d_final, axis=(0, 1))
    d_hidden = matmul("isd,fd->isf", d_final_low, fc2_weight)
    d_active = gelu_pull(d_hidden)[0]
    fc1_bias_grad = jnp.sum(d_active, axis=(0, 1))
    d_active_low = d_active.astype(b16)
    d_normed_two = matmul("isf,df->isd", d_active_low, fc1_weight)
    d_middle_norm, gain_two_grad, shift_two_grad = norm_pull_two(d_normed_two)
    d_middle = d_final + d_middle_norm
    d_middle_low = d_middle.astype(b16)
    proj_bias_grad = jnp.sum(d_middle, axis=(0, 1))
    d_heads = matmul("ise,de->isd", d_middle_low, proj_weight).astype(b16)
    d_heads_four = d_heads.reshape(item_count, half, HEADS, HEAD_DIM)
    d_probs = matmul("iqhd,ikhd->ihqk", d_heads_four, value_four)
    row_delta = jnp.sum(d_probs * attn_probs, axis=-1, keepdims=True)
    d_scores = (attn_probs * (d_probs - row_delta) * scale).astype(b16)
    d_query = matmul("ihqk,ikhd->iqhd", d_scores, key_four).reshape(item_count, half, width)
    d_key_all = matmul("ihqk,iqhd->ikhd", d_scores, query_four).reshape(
        item_count, slot_count, width
    )
    d_value_all = matmul("ihqk,iqhd->ikhd", probs_low, d_heads_four).reshape(
        item_count, slot_count, width
    )
    d_key_own, d_value_own = (
        lax.psum_scatter(
            d_key_all.astype(jnp.bfloat16), "seq", scatter_dimension=1, tiled=True
        ).astype(jnp.float32),
        lax.psum_scatter(
            d_value_all.astype(jnp.bfloat16), "seq", scatter_dimension=1, tiled=True
        ).astype(jnp.float32),
    )
    d_packed = jnp.concatenate([d_query, d_key_own, d_value_own], axis=-1).astype(b16)
    d_normed = matmul("ise,de->isd", d_packed, qkv_weight)
    d_base_norm, gain_one_grad, shift_one_grad = norm_pull_one(d_normed)
    d_base = d_middle + d_base_norm
    d_base_low = d_base.astype(b16)
    skip_bias_grad = jnp.sum(d_base, axis=(0, 1))
    d_joined = matmul("isd,cd->isc", d_base_low, skip_weight)
    tokens_grad = d_joined[..., :width].astype(b16)
    skip_part = d_joined[..., width:].astype(b16)
    skip_grad = lax.all_to_all(skip_part, "seq", split_axis=2, concat_axis=1, tiled=True)
    every_all = (
        lax.all_gather(joined, "seq", axis=1, tiled=True),
        lax.all_gather(d_base_low, "seq", axis=1, tiled=True),
        lax.all_gather(normed, "seq", axis=1, tiled=True),
        lax.all_gather(d_packed, "seq", axis=1, tiled=True),
        lax.all_gather(head_out, "seq", axis=1, tiled=True),
        lax.all_gather(d_middle_low, "seq", axis=1, tiled=True),
        lax.all_gather(normed_two, "seq", axis=1, tiled=True),
        lax.all_gather(d_active_low, "seq", axis=1, tiled=True),
        lax.all_gather(hidden, "seq", axis=1, tiled=True),
        lax.all_gather(d_final_low, "seq", axis=1, tiled=True),
    )
    skip_weight_grad, qkv_grad, proj_grad, fc1_grad, fc2_grad = (
        lax.psum_scatter(
            weight_rows(every_all[0], every_all[1], seq_pos, dp_count, seq_count),
            "dp",
            scatter_dimension=0,
            tiled=True,
        ),
        lax.psum_scatter(
            weight_rows(every_all[2], every_all[3], seq_pos, dp_count, seq_count),
            "dp",
            scatter_dimension=0,
            tiled=True,
        ),
        lax.psum_scatter(
            weight_rows(every_all[4], every_all[5], seq_pos, dp_count, seq_count),
            "dp",
            scatter_dimension=0,
            tiled=True,
        ),
        lax.psum_scatter(
            weight_rows(every_all[6], every_all[7], seq_pos, dp_count, seq_count),
            "dp",
            scatter_dimension=0,
            tiled=True,
        ),
        lax.psum_scatter(
            weight_rows(every_all[8], every_all[9], seq_pos, dp_count, seq_count),
            "dp",
            scatter_dimension=0,
            tiled=True,
        ),
    )
    vectors = (
        lax.psum_scatter(skip_bias_grad, ("dp", "seq"), scatter_dimension=0, tiled=True),
        lax.psum_scatter(gain_one_grad, ("dp", "seq"), scatter_dimension=0, tiled=True),
        lax.psum_scatter(shift_one_grad, ("dp", "seq"), scatter_dimension=0, tiled=True),
        lax.psum_scatter(proj_bias_grad, ("dp", "seq"), scatter_dimension=0, tiled=True),
        lax.psum_scatter(gain_two_grad, ("dp", "seq"), scatter_dimension=0, tiled=True),
        lax.psum_scatter(shift_two_grad, ("dp", "seq"), scatter_dimension=0, tiled=True),
        lax.psum_scatter(fc1_bias_grad, ("dp", "seq"), scatter_dimension=0, tiled=True),
        lax.psum_scatter(fc2_bias_grad, ("dp", "seq"), scatter_dimension=0, tiled=True),
    )
    return (
        block_out,
        tokens_grad,
        skip_grad,
        skip_weight_grad,
        vectors[0],
        vectors[1],
        vectors[2],
        qkv_grad,
        proj_grad,
        vectors[3],
        vectors[4],
        vectors[5],
        fc1_grad,
        vectors[6],
        fc2_grad,
        vectors[7],
    )


def solution(mesh):
    placed = (
        P("dp", "seq", None),
        P("dp", None, "seq"),
        P("dp"),
        P("dp", "seq", None),
        P(),
        P(),
        P(),
        P(),
        P(),
        P(),
        P(),
        P(),
        P(),
        P(),
        P(),
        P(),
        P(),
    )
    return jax.shard_map(
        shards,
        mesh=mesh,
        in_specs=placed,
        out_specs=(
            P("dp", "seq", None),
            P("dp", "seq", None),
            P("dp", None, "seq"),
            P(("dp", "seq"), None),
            P(("dp", "seq")),
            P(("dp", "seq")),
            P(("dp", "seq")),
            P(("dp", "seq"), None),
            P(("dp", "seq"), None),
            P(("dp", "seq")),
            P(("dp", "seq")),
            P(("dp", "seq")),
            P(("dp", "seq"), None),
            P(("dp", "seq")),
            P(("dp", "seq"), None),
            P(("dp", "seq")),
        ),
        check_vma=False,
    )
```

profile of v0, /device:TPU:0, one launch (start us, length us, event | category | flops | bytes accessed | tf_op | source)
XLA Modules:
  0.0 1012.8 jit_solution(10556658415052773637)
XLA Ops:
  47.6 18.6 %all_gather.36 = bf16[1,322,1152]{2,0,1:T(2,128)(2,1)} all-gather(bf16[1,161,1152]{2,0,1:T(2,128)(2,1)S(1)} %copy.91), channel_id=1, replica_groups=mesh['dp'=16,'seq'=2] {'seq'}, dimensions={1}, use_global_device_ids=true | all-gather | bytes 1112832 | tf_op jit(solution)/shard_map/all_gather | solution.py:87
  74.0 17.8 %all_gather.37 = bf16[1,322,1152]{2,0,1:T(2,128)(2,1)} all-gather(bf16[1,161,1152]{2,0,1:T(2,128)(2,1)S(1)} %copy.93), channel_id=1, replica_groups=mesh['dp'=16,'seq'=2] {'seq'}, dimensions={1}, use_global_device_ids=true | all-gather | bytes 1112832 | tf_op jit(solution)/shard_map/all_gather | solution.py:86
  105.7 12.4 %multiply_convert_fusion.1 = (bf16[161,4608]{1,0:T(8,128)(2,1)}, f32[161,4608]{1,0:T(8,128)S(1)}) fusion(f32[4608]{0:T(1024)S(1)} %copy-done.27, bf16[1152,4608]{1,0:T(8,128)(2,1)} %param.30, f32[161,1152]{1,0:T(8,128)S(1)} %get-tuple-element.60, f32[1152]{0:T(1024)S(1)} %convert_element_type.186, f32[1152]{0:T(1024)S(1)} %convert_element_type.185, ...), kind=kOutput, calls=%fused_computation.16 | convolution fusion | flops 1759201920 | bytes 15838984 | tf_op jit(solution)/shard_map/isd,df->isf/dot_general | solution.py:26
  118.2 10.6 %multiply_add_fusion = f32[161,4608]{1,0:T(8,128)S(1)} fusion(f32[161,4608]{1,0:T(8,128)S(1)} %get-tuple-element.62, bf16[4608,1152]{1,0:T(8,128)(2,1)S(1)} %bitcast.185, bf16[1,161,1152]{2,1,0:T(8,128)(2,1)S(1)} %copy-done.18), kind=kOutput, calls=%fused_computation.15 | convolution fusion | flops 1761984000 | bytes 16922880 | tf_op jit(solution)/shard_map/isd,fd->isf/dot_general | solution.py:26
  128.8 8.9 multiply_reduce_fusion.1
  150.4 21.0 %fusion.42 = bf16[16,72,322]{2,1,0:T(8,128)(2,1)} fusion(bf16[161,16,72]{0,2,1:T(8,128)(2,1)S(1)} %bitcast.183, f32[16,161,322]{2,1,0:T(8,128)} %fusion.95, f32[16,161,322]{2,1,0:T(8,128)} %get-tuple-element.58, f32[16,161]{1,0:T(8,128)S(1)} %get-tuple-element.57), kind=kOutput, calls=%fused_computation.58 | convolution fusion | flops 125624112 | bytes 7758912 | tf_op jit(solution)/shard_map/ihqk,iqhd->ikhd/dot_general | solution.py:26
  182.6 20.5 %fusion.45 = bf16[16,72,161]{2,1,0:T(8,128)(2,1)} fusion(bf16[322,16,72]{0,2,1:T(8,128)(2,1)S(1)} %bitcast.179, f32[16,161,322]{2,1,0:T(8,128)} %fusion.95, f32[16,161,322]{2,1,0:T(8,128)} %get-tuple-element.58, f32[16,161]{1,0:T(8,128)S(1)} %get-tuple-element.57), kind=kOutput, calls=%fused_computation.60 | convolution fusion | flops 125438640 | bytes 7758912 | tf_op jit(solution)/shard_map/ihqk,ikhd->iqhd/dot_general | solution.py:26
  203.1 24.8 %all-reduce.22.cloned.1.call-done = (bf16[1,322,1152]{1,2,0:T(8,128)(2,1)}, bf16[1,322,1152]{1,2,0:T(8,128)(2,1)}) async-done(((bf16[1,322,1152]{1,2,0:T(8,128)(2,1)}, bf16[1,322,1152]{1,2,0:T(8,128)(2,1)}), (bf16[1,322,1152]{1,2,0:T(8,128)(2,1)}, bf16[1,322,1152]{1,2,0:T(8,128)(2,1)})) %all-reduce.22.cloned.1.call-update) | async-done | bytes 1483792
  248.7 23.8 %all-gather.13.cloned.1.call-done = bf16[1,322,2304]{2,0,1:T(2,128)(2,1)} async-done(((bf16[1,161,2304]{2,0,1:T(2,128)(2,1)}), bf16[1,322,2304]{2,0,1:T(2,128)(2,1)}) %all-gather.13.cloned.1.call-update) | async-done | bytes 1483792 | tf_op jit(solution)/shard_map/all_gather | solution.py:152
  278.5 32.9 %all_gather.39 = bf16[1,322,1152]{2,0,1:T(2,128)(2,1)S(1)} all-gather(bf16[1,161,1152]{2,0,1:T(2,128)(2,1)} %copy.104), channel_id=1, replica_groups=mesh['dp'=16,'seq'=2] {'seq'}, dimensions={1}, use_global_device_ids=true | all-gather | bytes 1112832 | tf_op jit(solution)/shard_map/all_gather | solution.py:153
  316.9 30.0 %all_gather.47 = bf16[1,322,1152]{2,0,1:T(2,128)(2,1)} all-gather(bf16[1,161,1152]{2,0,1:T(2,128)(2,1)S(1)} %copy.112), channel_id=1, replica_groups=mesh['dp'=16,'seq'=2] {'seq'}, dimensions={1}, use_global_device_ids=true | all-gather | bytes 1112832 | tf_op jit(solution)/shard_map/all_gather | solution.py:161
  346.9 12.5 %reshape.624 = bf16[1,322,16,2,144]{4,3,2,1,0:T(2,128)(2,1)} reshape(bf16[2,161,4608]{2,1,0:T(8,128)(2,1)} %all-gather.19.cloned.1.call-done) | data formatting | bytes 5935104 | tf_op jit(solution)/shard_map/reshape | solution.py:32
  367.1 9.5 copy.125
  389.1 24.5 %all_gather.42 = bf16[1,322,1152]{2,0,1:T(2,128)(2,1)S(1)} all-gather(bf16[1,161,1152]{2,0,1:T(2,128)(2,1)S(1)} %copy.107), channel_id=1, replica_groups=mesh['dp'=16,'seq'=2] {'seq'}, dimensions={1}, use_global_device_ids=true | all-gather | bytes 1112832 | tf_op jit(solution)/shard_map/all_gather | solution.py:156
  416.2 18.4 %all-gather.5 = bf16[2,161,1152]{2,1,0:T(8,128)(2,1)S(1)} all-gather(bf16[1,161,1152]{2,1,0:T(8,128)(2,1)} %get-tuple-element.51), channel_id=3, replica_groups=mesh['dp'=16,'seq'=2] {'seq'}, dimensions={0}, use_global_device_ids=true | all-gather | bytes 1112832 | tf_op jit(solution)/shard_map/all_gather | solution.py:158
  439.8 34.5 %all_gather.43 = bf16[1,322,1152]{2,0,1:T(2,128)(2,1)S(1)} all-gather(bf16[1,161,1152]{2,0,1:T(2,128)(2,1)S(1)} %copy-done.13), channel_id=1, replica_groups=mesh['dp'=16,'seq'=2] {'seq'}, dimensions={1}, use_global_device_ids=true | all-gather | bytes 1112832 | tf_op jit(solution)/shard_map/all_gather | solution.py:157
  475.3 12.0 %all-gather.4 = bf16[2,161,1152]{2,1,0:T(8,128)(2,1)} all-gather(bf16[1,161,1152]{2,1,0:T(8,128)(2,1)S(1)} %copy-done.17), channel_id=2, replica_groups=mesh['dp'=16,'seq'=2] {'seq'}, dimensions={0}, use_global_device_ids=true | all-gather | bytes 1112832 | tf_op jit(solution)/shard_map/all_gather | solution.py:154
  507.4 9.0 fusion.96
  524.3 304.5 %fusion.87 = (f32[48,3456]{1,0:T(8,128)S(1)}, f32[48,1152]{1,0:T(8,128)S(1)}, f32[40,4608]{1,0:T(8,128)}) fusion(f32[576,3456]{1,0:T(8,128)} %fusion.28, f32[576,1152]{1,0:T(8,128)S(1)} %fusion.58, f32[576,4608]{1,0:T(8,128)} %fusion.96), kind=kCustom, calls=%all-reduce-scatter.3 | all-reduce-scatter fusion | flops 6488066 | bytes 22856192
  829.5 10.3 %collective-permute-start.6 = (f32[48,1152]{1,0:T(8,128)S(1)}, f32[48,1152]{1,0:T(8,128)}, u32[]{:S(2)}, u32[]{:S(2)}) collective-permute-start(f32[48,1152]{1,0:T(8,128)S(1)} %get-tuple-element.39), channel_id=1, source_target_pairs={{0,6},{2,8},{4,10},{6,12},{8,14},{10,16},{12,18},{14,20},{16,22},{... | collective-permute-start | bytes 663560
  839.8 9.8 collective-permute-start.5
  895.3 52.2 %all-reduce.17 = (f32[1152]{0:T(1024)S(1)}, f32[1152]{0:T(1024)S(1)}, f32[1152]{0:T(1024)S(1)}, f32[1152]{0:T(1024)S(1)}, f32[1152]{0:T(1024)S(1)}, /*index=5*/f...) all-reduce(f32[1152]{0:T(1024)S(1)} %copy-done.25, ...), channel_id=9, replica_groups=mesh['dp'=16,'seq'=2] {'dp','seq'}, use_global_device_ids=true, to_apply=%region_15.16.clone | all-reduce | flops 12672 | bytes 101376
  970.8 19.6 %concatenate.34 = f32[228,3456]{1,0:T(8,128)} concatenate(f32[36,3456]{1,0:T(8,128)} %collective-permute-done.3, f32[48,3456]{1,0:T(8,128)} %copy-done.21, f32[48,3456]{1,0:T(8,128)} %collective-permute-done.1, f32[48,3456]{1,0:T(8,128)} %collective-permute-done, f32[48,3456]{1,0:T(8,128)S(1)} %get-tuple-element.38), dimensions={0} | concatenate | bytes 6303744
  992.3 11.4 %concatenate.36 = f32[100,4608]{1,0:T(8,128)} concatenate(f32[20,4608]{1,0:T(8,128)} %collective-permute-done.9, f32[40,4608]{1,0:T(8,128)} %collective-permute-done.8, f32[40,4608]{1,0:T(8,128)} %get-tuple-element.40), dimensions={0} | concatenate | bytes 3686400
  (245 shorter events, 245.5 us)
Async XLA Ops:
  7.2 97.3 %copy-start = (bf16[1152,1152]{1,0:T(8,128)(2,1)S(1)}, bf16[1152,1152]{1,0:T(8,128)(2,1)}, u32[]{:S(2)}) copy-start(bf16[1152,1152]{1,0:T(8,128)(2,1)} %param.26) | copy-start | bytes 7962628
  16.1 12.1 %all-to-all-start = ((bf16[2,2,46368]{2,1,0:T(2,128)(2,1)}), bf16[2,2,46368]{2,1,0:T(2,128)(2,1)}, u32[]{:S(2)}, u32[]{:S(2)}) async-start(bf16[2,2,46368]{2,1,0:T(2,128)(2,1)} %reshape.636), calls=%async_computation | async-start | bytes 743424 | tf_op jit(solution)/shard_map/all_to_all | solution.py:76
  20.3 207.6 %all-reduce.22.cloned.1.call-start = ((), (), s32[]{:S(2)}) async-start(), calls=%async_computation.10 | async-start | bytes 3538944
  105.4 32.3 %copy-start.3 = (f32[161,1152]{1,0:T(8,128)}, f32[161,1152]{1,0:T(8,128)S(1)}, u32[]{:S(2)}) copy-start(f32[161,1152]{1,0:T(8,128)S(1)} %get-tuple-element.60) | copy-start | bytes 2225668
  171.4 101.0 %all-gather.13.cloned.1.call-start = ((), (), s32[]{:S(2)}) async-start(), calls=%async_computation.4 | async-start | bytes 4451328 | tf_op jit(solution)/shard_map/all_gather | solution.py:152
  174.9 172.0 %all-gather.19.cloned.1.call-start = ((), (), s32[]{:S(2)}) async-start(), calls=%async_computation.8 | async-start | bytes 4644864 | tf_op jit(solution)/shard_map/all_gather | solution.py:160
  175.7 327.4 %all-gather.17.cloned.1.call-start = ((), (), s32[]{:S(2)}) async-start(), calls=%async_computation.7 | async-start | bytes 4644864 | tf_op jit(solution)/shard_map/all_gather | solution.py:159
  181.3 335.2 %all-gather.15.cloned.1.call-start = ((), (), s32[]{:S(2)}) async-start(), calls=%async_computation.5 | async-start | bytes 6676992 | tf_op jit(solution)/shard_map/all_gather | solution.py:155
  236.9 768.8 %reduce-scatter.15.cloned.1.call-start = ((), (), s32[]{:S(2)}) async-start(), calls=%async_computation.9 | async-start | bytes 5640192
  315.4 690.4 %reduce-scatter.13.cloned.1.call-start = ((), (), s32[]{:S(2)}) async-start(), calls=%async_computation.6 | async-start | bytes 11280384 | tf_op jit(solution)/shard_map/reduce_scatter | solution.py:188
  439.8 35.4 %copy-start.17 = (bf16[1,161,1152]{2,1,0:T(8,128)(2,1)S(1)}, bf16[1,161,1152]{2,1,0:T(8,128)(2,1)}, u32[]{:S(2)}) copy-start(bf16[1,161,1152]{2,1,0:T(8,128)(2,1)} %get-tuple-element.52) | copy-start | bytes 1112836
  829.5 50.3 %collective-permute-start.6 = (f32[48,1152]{1,0:T(8,128)S(1)}, f32[48,1152]{1,0:T(8,128)}, u32[]{:S(2)}, u32[]{:S(2)}) collective-permute-start(f32[48,1152]{1,0:T(8,128)S(1)} %get-tuple-element.39), channel_id=1, source_target_pairs={{0,6},{2,8},{4,10},{6,12},{8,14},{10,16},{12,18},{14,20},{16,22},{... | collective-permute-start | bytes 663560
  839.8 42.4 %collective-permute-start.5 = (f32[48,1152]{1,0:T(8,128)S(1)}, f32[48,1152]{1,0:T(8,128)}, u32[]{:S(2)}, u32[]{:S(2)}) collective-permute-start(f32[48,1152]{1,0:T(8,128)S(1)} %get-tuple-element.39), channel_id=1, source_target_pairs={{0,4},{2,6},{4,8},{6,10},{8,12},{10,14},{12,16},{14,18},{16,20},{1... | collective-permute-start | bytes 663560
  849.7 34.7 %collective-permute-start.4 = (f32[48,1152]{1,0:T(8,128)S(1)}, f32[48,1152]{1,0:T(8,128)}, u32[]{:S(2)}, u32[]{:S(2)}) collective-permute-start(f32[48,1152]{1,0:T(8,128)S(1)} %get-tuple-element.39), channel_id=1, source_target_pairs={{0,2},{2,4},{4,6},{6,8},{8,10},{10,12},{12,14},{14,16},{16,18},{18... | collective-permute-start | bytes 663560
  852.7 23.9 %collective-permute-start.7 = (f32[36,1152]{1,0:T(8,128)}, f32[36,1152]{1,0:T(8,128)}, u32[]{:S(2)}, u32[]{:S(2)}) collective-permute-start(f32[36,1152]{1,0:T(8,128)} %slice.28), channel_id=1, source_target_pairs={{0,8},{2,10},{4,12},{6,14},{8,16},{10,18},{12,20},{14,22},{16,24},... | collective-permute-start | bytes 497672
  857.5 30.4 %copy-start.34 = (f32[1152]{0:T(1024)S(1)}, f32[1152]{0:T(1024)}, u32[]{:S(2)}) copy-start(f32[1152]{0:T(1024)} %convert_element_type.190) | copy-start | bytes 13828
  869.1 83.2 %all-to-all-start.1 = ((bf16[2,2,46368]{2,1,0:T(2,128)(2,1)}), bf16[2,2,46368]{2,1,0:T(2,128)(2,1)S(1)}, u32[]{:S(2)}, u32[]{:S(2)}) async-start(bf16[2,2,46368]{2,1,0:T(2,128)(2,1)} %reshape.638), calls=%async_computation.1 | async-start | bytes 743424 | tf_op jit(solution)/shard_map/all_to_all | solution.py:150
  873.5 96.5 %collective-permute-start.2 = (f32[48,3456]{1,0:T(8,128)S(1)}, f32[48,3456]{1,0:T(8,128)S(1)}, u32[]{:S(2)}, u32[]{:S(2)}) collective-permute-start(f32[48,3456]{1,0:T(8,128)S(1)} %get-tuple-element.38), channel_id=1, source_target_pairs={{0,6},{2,8},{4,10},{6,12},{8,14},{10,16},{12,18},{14,20},{16,22},{... | collective-permute-start | bytes 1990664
  876.7 93.3 %collective-permute-start.1 = (f32[48,3456]{1,0:T(8,128)S(1)}, f32[48,3456]{1,0:T(8,128)}, u32[]{:S(2)}, u32[]{:S(2)}) collective-permute-start(f32[48,3456]{1,0:T(8,128)S(1)} %get-tuple-element.38), channel_id=1, source_target_pairs={{0,4},{2,6},{4,8},{6,10},{8,12},{10,14},{12,16},{14,18},{16,20},{1... | collective-permute-start | bytes 1990664
  879.8 90.9 %collective-permute-start = (f32[48,3456]{1,0:T(8,128)S(1)}, f32[48,3456]{1,0:T(8,128)}, u32[]{:S(2)}, u32[]{:S(2)}) collective-permute-start(f32[48,3456]{1,0:T(8,128)S(1)} %get-tuple-element.38), channel_id=1, source_target_pairs={{0,2},{2,4},{4,6},{6,8},{8,10},{10,12},{12,14},{14,16},{16,18},{18... | collective-permute-start | bytes 1990664
  882.3 82.7 %collective-permute-start.3 = (f32[36,3456]{1,0:T(8,128)}, f32[36,3456]{1,0:T(8,128)}, u32[]{:S(2)}, u32[]{:S(2)}) collective-permute-start(f32[36,3456]{1,0:T(8,128)} %slice.27), channel_id=1, source_target_pairs={{0,8},{2,10},{4,12},{6,14},{8,16},{10,18},{12,20},{14,22},{16,24},... | collective-permute-start | bytes 1493000
  884.4 107.8 %collective-permute-start.8 = (f32[40,4608]{1,0:T(8,128)}, f32[40,4608]{1,0:T(8,128)}, u32[]{:S(2)}, u32[]{:S(2)}) collective-permute-start(f32[40,4608]{1,0:T(8,128)} %get-tuple-element.40), channel_id=1, source_target_pairs={{0,2},{2,4},{4,6},{6,8},{8,10},{10,12},{12,14},{14,16},{16,18},{18... | collective-permute-start | bytes 2211848
  965.0 27.3 %collective-permute-start.9 = (f32[20,4608]{1,0:T(8,128)}, f32[20,4608]{1,0:T(8,128)}, u32[]{:S(2)}, u32[]{:S(2)}) collective-permute-start(f32[20,4608]{1,0:T(8,128)} %slice.29), channel_id=1, source_target_pairs={{0,4},{2,6},{4,8},{6,10},{8,12},{10,14},{12,16},{14,18},{16,20},{1... | collective-permute-start | bytes 1105928
  970.8 35.0 %copy-start.1 = (bf16[1152,1152]{1,0:T(8,128)(2,1)S(1)}, bf16[1152,1152]{1,0:T(8,128)(2,1)}, u32[]{:S(2)}) copy-start(bf16[1152,1152]{1,0:T(8,128)(2,1)} %param.26) | copy-start | bytes 7962628
  (42 other events, 386.9 us)
Sparse Core Ops, SparseCore 0:
  171.6 56.2 all-reduce.21
  229.5 42.9 all-gather.12
  274.1 69.6 all-gather.18
  345.2 44.3 all-gather.16
  391.1 93.1 all-gather.14
  489.3 124.0 reduce-scatter.14
  618.5 174.7 reduce-scatter.12
where the time goes:
time: 1020 us; the launch traced here: 1010 us
  blocking collectives  545 us (53%)
  local copies, waits for them, and re-layouts  169 us (17%)
  matrix products  151 us (15%)
  starting transfers between devices  53.9 us (5%)
  waiting for transfers between devices  52.6 us (5%)
  other arithmetic  23.7 us (2%)
  between operations  17.7 us (2%)
    unnamed x2, blocking collectives  357 us
    dot_general x20, matrix products, matmul(): return jnp.einsum(form, left, right, preferred_element_type=jnp.float32)  146 us
    unnamed x123, local copies, waits for them, and re-layouts  83 us
    unnamed x12, starting transfers between devices  46 us
    all_gather x1, blocking collectives, shards(): lax.all_gather(d_middle_low, 'seq', axis=1, tiled=True)  34.5 us
    all_gather x1, blocking collectives, shards(): lax.all_gather(d_base_low, 'seq', axis=1, tiled=True)  32.9 us
    all_gather x1, blocking collectives, shards(): lax.all_gather(d_final_low, 'seq', axis=1, tiled=True)  30 us
    unnamed x19, waiting for transfers between devices  25.6 us
  transfers between devices with their start and end apart: 19, of which 3 were waited for; matrix products, arithmetic and copies ran while one was open for 52% of the time, Pallas kernels for 0%

commit v1 on v0

v1 whole, which is shorter than its diff:
```python
import functools
import types

import jax
import jax.numpy as jnp
from jax import lax
from jax.experimental import pallas as pl
from jax.experimental.pallas import tpu as pltpu
from jax.sharding import PartitionSpec as P

HEADS = 16
HEAD_DIM = 72
NORM_EPS = 1e-05
MASKED = -1e30
LANE = 128
TILE = 384
ROWS = 32
F32 = jnp.float32
B16 = jnp.bfloat16
MESH = pl.DeviceIdType.MESH
VMEM_BYTES = 64 * 1024 * 1024


def up(n, m):
    return -(-n // m) * m


def mm(a, b):
    return lax.dot_general(a, b, (((1,), (0,)), ((), ())), preferred_element_type=F32)


def mm_nt(a, b):
    return lax.dot_general(a, b, (((1,), (1,)), ((), ())), preferred_element_type=F32)


def mm_tn(a, b):
    return lax.dot_general(a, b, (((0,), (0,)), ((), ())), preferred_element_type=F32)


def iota(shape, dim):
    return lax.broadcasted_iota(jnp.int32, shape, dim)


def onehot(mask):
    return jnp.where(mask, 1.0, 0.0).astype(B16)


def rows_of(i, n=ROWS):
    return pl.ds(pl.multiple_of(i * n, n), n)


def lanes_of(i, n=TILE):
    return pl.ds(pl.multiple_of(i * n, LANE), n)


def loop(n, body, unroll=1, first=0):
    lax.fori_loop(first, first + n, lambda i, _: (body(i), None)[1], None, unroll=unroll)


def sizes(half, width, hidden_width, dp_count):
    z = types.SimpleNamespace()
    z.half, z.D, z.FF = half, width, hidden_width
    z.HP = up(half, 16)
    z.S = 2 * z.HP
    z.SP = up(z.S, LANE)
    z.FH = hidden_width // 2
    z.DH = width // 2
    z.WS = z.DH // LANE * LANE
    z.LO = z.DH - z.WS
    z.W = width - z.WS
    z.HN = HEADS // 2
    z.HS = z.HN // 2 * HEAD_DIM
    z.SW = z.HS // LANE * LANE
    z.SL = up(z.HS + z.LO + z.HS - z.SW, LANE)
    z.PQ = up(3 * z.HS, LANE)
    z.QN = dp_count // 2
    z.QH = z.QN // 2
    z.QP = z.QN // 4
    z.bits = z.QN.bit_length() - 1
    z.far = z.bits > 3
    z.NB = 2 * z.QN
    blocks = 4 * z.QN
    z.r2, z.rs, z.rp, z.r1 = hidden_width // blocks, 2 * width // blocks, width // blocks, width // z.QN
    z.r2p, z.rsp, z.rpp, z.r1p = (up(v, 16) for v in (z.r2, z.rs, z.rp, z.r1))
    return z


def transpose_block(src, block, r, rp, shift, sp, total):
    span = min(up(r + LANE - 1, LANE), total)
    first = shift + block * r
    start = jnp.minimum(first // LANE * LANE, total - span)
    start = pl.multiple_of(start, LANE)
    row, lane = iota((rp, span), 0), iota((rp, span), 1)
    pick = onehot((lane == row + (first - start)) & (row < r))
    return mm_nt(pick, src[0:sp, pl.ds(start, span)]).astype(B16)


def jobs_of(z):
    rest = list(range(2, z.bits))
    near, far = [0, 1, *rest], [1, 0, *rest]
    jobs, base = [], 0
    for name, group, r, rp, start, n, w, parts, order in (
        ("2a", "2", z.r2, z.r2p, 0, 2 * TILE, TILE, 1, near),
        ("2b", "2", z.r2, z.r2p, 2 * TILE, z.D - 2 * TILE, TILE, 1, far),
        ("1a", "1", z.r1, z.r1p, 0, 2 * TILE, TILE, 1, near),
        ("1b", "1", z.r1, z.r1p, 2 * TILE, z.FH // 2 - 2 * TILE, TILE, 1, far),
        ("p", "p", z.rp, z.rpp, 0, z.D, TILE, 1, far),
        ("qa", "q", z.r1, z.r1p, 0, 512, 512, 1, near),
        ("qb", "q", z.r1, z.r1p, 512, z.PQ - 512, TILE, 1, far),
        ("s", "s", z.rs, z.rsp, 0, z.D, TILE, 1, near),
    ):
        jobs.append(
            types.SimpleNamespace(
                name=name, group=group, r=r, rp=rp, start=start, n=n, w=w, nt=n // w, parts=parts, order=order, base=base
            )
        )
        base += n // w * parts
    return jobs, base


GROUPS = "21pqs"


def landing_of(z):
    return {
        f"rv{j.name}{s}": ((j.nt,) + (2,) * (z.bits - 1 - s) + (j.rp, j.w), z.far and s > 0)
        for j in jobs_of(z)[0]
        for s in range(z.bits)
    }


INS = (
    "lens", "tok", "sk", "cot", "sb", "g1", "h1", "pb", "g2", "h2", "b1", "b2", "sw", "qw", "pw", "f1", "f2",
)
LEFT_OUTS = ("LT2", "LT1", "LTq", "LTp", "LTs", "R1", "Rp", "Rq")


def any_outs(z):
    return LEFT_OUTS + tuple(n for n, (_, out) in landing_of(z).items() if out)


VMEM_OUTS = ("bo", "tg", "sg", "w2", "w1", "wp", "wq", "ws", "vout")


def out_shapes(z):
    s = jax.ShapeDtypeStruct
    landing = {n: s(shape, B16) for n, (shape, _) in landing_of(z).items()}
    left = lambda rows: s((2, 2, 2, z.QP, rows, z.SP), B16)
    return landing | dict(
        LT2=left(z.r2p),
        LT1=left(z.r1p),
        LTq=left(z.r1p),
        LTp=left(z.rpp),
        LTs=left(z.rsp),
        R1=s((2, z.S, z.FH // 2), B16),
        Rp=s((2, z.S, z.D), B16),
        Rq=s((2, z.S, z.PQ), B16),
        bo=s((z.half, z.D), B16),
        tg=s((z.half, z.D), B16),
        sg=s((2 * z.half, z.DH), B16),
        w2=s((z.r2, z.D), F32),
        w1=s((z.r1 // 4, z.FF), F32),
        wp=s((z.rp, z.D), F32),
        wq=s((z.r1 // 4, 3 * z.D), F32),
        ws=s((z.rs, z.D), F32),
        vout=s((16, z.D), F32),
    )


def scratch_of(z):
    v, dma = pltpu.VMEM, pltpu.SemaphoreType.DMA
    jobs, tiles = jobs_of(z)
    fp = up(z.r1 // 4, 8)
    out = dict(
        tokin=v((2, z.HP, z.D), B16),
        skin=v((2, z.S, z.W), B16),
        lent=v((2, 8, LANE), F32),
        dfin=v((2, z.S, z.D), B16),
        acc0=v((z.S, z.D), F32),
        acc1=v((z.S, z.D), F32),
        acc2=v((z.S, z.D), F32),
        acc3=v((z.HP, z.D), F32),
        psend=v((z.D // TILE, z.S, TILE), B16),
        pin0=v((z.D // TILE, z.S, TILE), B16),
        pin1=v((z.D // TILE, z.S, TILE), B16),
        pin3=v((z.HP, z.D), B16),
        pk=v((z.S, 3 * z.W), B16),
        probs=v((z.HN, z.S, z.S), B16),
        dact=v((z.S, z.FH), B16),
        dbase=v((2, z.S, z.D), B16),
        st2=v((4, 2, z.QP, z.r2p, z.SP), B16),
        st1=v((2, 2, z.QP, z.r1p, z.SP), B16),
        heads=v((z.SP, z.W), B16),
        bosum=v((z.HP, z.D), B16),
        rowv=v((8, z.D), F32),
        b1v=v((1, z.FF), F32),
        fbias=v((1, z.FH), F32),
        vb=v((3 + z.bits, 16, z.D), F32),
        vr=v((2 + z.bits, 16, z.D), F32),
    )
    for n, (shape, outside) in landing_of(z).items():
        if not outside:
            out[n] = v(shape, B16)
    for n, cols in (("1", z.FH // 2), ("q", z.PQ)):
        out["fr" + n] = v((4, fp, cols), F32)
    out["wsem"] = dma((12,))
    out["lsem"] = dma((16,))
    out["ssem"], out["rsem"] = dma((64,)), dma((64,))
    out["semld"] = dma((len(GROUPS), 6))
    out["semgs"], out["semgr"] = dma((z.bits, tiles)), dma((z.bits, tiles))
    out["semfs"], out["semfr"] = dma((2, 4)), dma((2, 4))
    out["semvs"], out["semvr"] = dma((2 + z.bits,)), dma((2 + z.bits,))
    return out


def scope_one(z):
    v = pltpu.VMEM
    return dict(
        qwv=v((z.D, 3 * z.W), B16),
        pwv=v((z.W, z.D), B16),
        f1v=v((z.D, z.FH), B16),
        f2v=v((z.FH, z.D), B16),
        atile=v((z.S, TILE), F32),
        hidden=v((z.SP, z.FH), B16),
        normed=v((z.SP, z.D), B16),
        normed2=v((z.SP, z.D), B16),
        stq=v((2, 2, z.QP, z.r1p, z.SP), B16),
        sts=v((4, 2, z.QP, z.rsp, z.SP), B16),
    )


def scope_start(z):
    v = pltpu.VMEM
    return dict(
        tokpad=v((z.HP, z.D), B16),
        skpad=v((z.S, z.W), B16),
        xin=v((z.SP, z.D), B16),
    )


def scope_two(z):
    v = pltpu.VMEM
    jobs, _ = jobs_of(z)
    out = dict(
        dmidl=v((z.S, z.D), B16),
        dpack=v((z.S, 3 * z.W), B16),
        slab=v((2, z.S, z.PQ), B16),
        stp=v((4, 2, z.QP, z.rpp, z.SP), B16),
        slotl=v((1, 2, 2, 2, z.QP, max(z.r1p, z.r2p, z.rsp), z.SP), B16),
        slotr=v((1, 2 * z.SP, z.D), B16),
    )
    if z.far:
        out["zin"] = v((z.QP, max(j.rp for j in jobs), 512), B16)
    for j in jobs:
        out["pr" + j.name] = v((j.nt,) + (2,) * z.bits + (j.rp, j.w), B16)
    return out


def scope_back(z):
    v = pltpu.VMEM
    return dict(qwb=v((z.D, 3 * z.W), B16), pwb=v((z.W, z.D), B16))


def scope_end(z):
    v = pltpu.VMEM
    fp = up(z.r1 // 4, 8)
    return dict(
        swb=v((z.D, z.D), B16),
        sumt=v((z.r1p, 512), F32),
        fs1=v((4, fp, z.FH // 2), F32),
        fsq=v((4, fp, z.PQ), F32),
    )


def kernel(z, *refs):
    scratch = scratch_of(z)
    r = types.SimpleNamespace(**dict(zip((*INS, *any_outs(z), *VMEM_OUTS, *scratch), refs, strict=True)))
    jobs, _ = jobs_of(z)
    j2a, j2b, j1a, j1b, jp, jqa, jqb, js = jobs
    d, x = lax.axis_index("dp"), lax.axis_index("seq")
    c, q = lax.rem(d, 2), d // 2
    bit = [lax.rem(q // 2**b, 2) for b in range(z.bits)]
    me = 2 * c + x
    peer, xpeer = (d + 1 - 2 * c, x), (d, 1 - x)
    across = [(d + (1 - 2 * bit[b]) * 2 ** (b + 1), x) for b in range(z.bits)]
    D, S, HP, half = z.D, z.S, z.HP, z.half
    nt = D // TILE

    def scoped(spec, body):
        def inner(*held):
            for name, ref in zip(spec, held, strict=True):
                setattr(r, name, ref)
            body()
            for name in spec:
                delattr(r, name)

        pl.run_scoped(inner, *spec.values())

    def quad(k):
        return (2 * q + k // 2, lax.rem(k, 2))

    def copy_to(src, dst, ss, rs, dev):
        return pltpu.make_async_remote_copy(
            src_ref=src, dst_ref=dst, send_sem=ss, recv_sem=rs, device_id=dev, device_id_type=MESH
        )

    used = [0]

    def slots(n):
        used[0] += n
        return used[0] - n

    def remote(src, dst, slot, dev):
        return copy_to(src, dst, r.ssem.at[slot], r.rsem.at[slot], dev)

    def wait_recv(dst, slot):
        remote(dst, dst, slot, xpeer).wait_recv()

    def wait_send(src, slot):
        remote(src, src, slot, xpeer).wait_send()

    def local(src, dst, n):
        return pltpu.make_async_copy(src, dst, r.lsem.at[n])

    def load(src, dst, n):
        return pltpu.make_async_copy(src, dst, r.wsem.at[n])

    def at16(start, n):
        return pl.ds(pl.multiple_of(start, 16), n)

    def at128(start, n):
        return pl.ds(pl.multiple_of(start, LANE), n)

    hx, hx1, hc, hc1 = (at16(HP * v, HP) for v in (x, 1 - x, c, 1 - c))

    S_LEN, S_TOK, S_SK, S_COT, S_P0, S_P1, S_P2, S_P4 = (slots(n) for n in (1, 2, 2, 3, nt, nt, nt, nt))
    S_P3, S_TS, S_TP, S_T2, S_XQ, S_X1, S_XP, S_XS, S_R1, S_RQ, S_BO = (
        slots(n) for n in (1, 3, 3, 6, 2, 2, 2, 2, 1, 1, 1)
    )

    barrier = pltpu.get_barrier_semaphore()
    for t in range(1, 4):
        pl.semaphore_signal(barrier, inc=1, device_id=quad(lax.rem(me + t, 4)), device_id_type=MESH)
    for other in across:
        pl.semaphore_signal(barrier, inc=1, device_id=other, device_id_type=MESH)
    pl.semaphore_wait(barrier, 3 + z.bits)

    def qkv_loads(dst):
        return [
            load(r.qw.at[:, at128(D * j + z.WS * c, z.W)], dst.at[:, z.W * j : z.W * (j + 1)], 1 + j) for j in range(3)
        ]

    def proj_load(dst):
        return load(r.pw.at[at16(z.WS * c, z.W), :], dst, 4)

    def partial_sums(value, mine, theirs, slot):
        def step(i):
            v = value(i)
            at = lanes_of(i)
            mine[:, at] = v
            r.psend[i] = v.astype(B16)
            remote(r.psend.at[i], theirs.at[i], slot + i, peer).start()

        loop(nt, step)

    def partial_done(theirs, slot):
        def step(i):
            remote(r.psend.at[i], theirs.at[i], slot + i, peer).wait()

        loop(nt, step)

    def spread_blocks(src, stage, rr, rrp, shift, out, slot, lslot, part=0, parts=1):
        n = z.NB // parts
        known = src.shape[1] * (part + 1) // parts

        def step(b):
            m = b // 4
            stage[lax.rem(b, 4), m // z.QP, lax.rem(m, z.QP)] = transpose_block(src, b, rr, rrp, shift, z.SP, known)

        loop(n, step, 4, part * n)
        some = slice(part, part + 1) if parts > 1 else slice(0, 2)
        for t in range(1, 4):
            k = lax.rem(me + t, 4)
            remote(stage.at[k, some], out.at[x, c, some], slot + part * 3 + t - 1, quad(k)).start()
        local(stage.at[me, some], out.at[x, c, some], lslot + part).start(priority=1)

    def spread_sent(stage, out, slot, lslot, parts=1):
        n = 2 // parts
        for i in range(3 * parts):
            wait_send(stage.at[0, 0:n], slot + i)
        for part in range(parts):
            local(stage.at[0, 0:n], out.at[x, 0, 0:n], lslot + part).wait()

    def spread_here(out, slot, part=0, parts=1):
        for i in range(3):
            wait_recv(out.at[x, 0, 0 : 2 // parts], slot + part * 3 + i)

    def whole_blocks(src, stage, out, slot, lslot):
        def step(b):
            stage[b // (2 * z.QP), lax.rem(b // z.QP, 2), lax.rem(b, z.QP)] = transpose_block(
                src, b, z.r1, z.r1p, 0, z.SP, D
            )

        loop(z.QN, step, 4)
        remote(stage.at[c], out.at[x, c], slot, xpeer).start()
        local(stage, out.at[x], lslot).start(priority=1)

    def relay(out, part, slot):
        wait_recv(out.at[1 - x, part], slot)
        remote(out.at[1 - x, part], out.at[1 - x, part], slot + 1, peer).start()

    def whole(tiles, at):
        return jnp.concatenate([tiles[t, at] for t in range(nt)], axis=1).astype(F32)

    def normalise(v, gain, shift):
        mean = jnp.mean(v, axis=-1, keepdims=True)
        centred = v - mean
        var = jnp.mean(centred * centred, axis=-1, keepdims=True)
        return centred * lax.rsqrt(var + NORM_EPS) * gain + shift

    def norm_back(v, dn, gain):
        mean = jnp.mean(v, axis=-1, keepdims=True)
        centred = v - mean
        var = jnp.mean(centred * centred, axis=-1, keepdims=True)
        rstd = lax.rsqrt(var + NORM_EPS)
        hat = centred * rstd
        dh = dn * gain
        one = jnp.mean(dh, axis=-1, keepdims=True)
        two = jnp.mean(dh * hat, axis=-1, keepdims=True)
        return rstd * (dh - one - hat * two), dn * hat

    def fold(v):
        return jnp.sum(v, axis=0, keepdims=True)

    zero = jnp.zeros((1, D), F32)
    SB, G1, H1, PB, G2, H2, B2 = range(7)

    def rowp(i):
        return r.rowv[i : i + 1, :]

    tok_self, sk_self = (c == 0) & (x == 0), (c == 1) & (x == 1)
    span = 2 * LANE
    scale = HEAD_DIM ** (-0.5)

    def head_window(h):
        first = z.LO * c + HEAD_DIM * h
        start = pl.multiple_of(jnp.minimum(first // LANE * LANE, z.W - span), LANE)
        lane = iota((1, span), 1) + start
        keep = jnp.where((lane >= first) & (lane < first + HEAD_DIM), 1.0, 0.0)
        return start, keep

    def length_here():
        return jnp.where(c == x, r.lent[0], r.lent[1])[0:1, 0:1]

    def begin():
        load(r.sw.at[at16(D * c, D)], r.f1v.at[:, 0:D], 0).start(priority=1)
        for v in qkv_loads(r.qwv):
            v.start(priority=1)
        proj_load(r.pwv).start(priority=1)
        length = r.lens[0].astype(F32)
        r.lent[0] = jnp.full((8, LANE), length, F32)
        remote(r.lent.at[0], r.lent.at[1], S_LEN, peer).start()
        spread = onehot((iota((HP, half), 0) == iota((HP, half), 1)))
        r.tokpad[...] = mm(spread, r.tok[...]).astype(B16)

        @pl.when(tok_self)
        def _():
            r.tokin[x] = r.tokpad[...]

        @pl.when(jnp.logical_not(tok_self))
        def _():
            remote(r.tokpad, r.tokin.at[x], S_TOK + x, quad(c)).start()

        row, col = iota((S, 2 * half), 0), iota((S, 2 * half), 1)
        pick = onehot(((row < half) & (row == col)) | ((row >= HP) & (row < HP + half) & (col == row - (HP - half))))
        shift = onehot(iota((z.DH, z.W), 1) == iota((z.DH, z.W), 0) + z.LO * x)
        r.skpad[...] = mm(mm(pick, r.sk[...]).astype(B16), shift).astype(B16)

        @pl.when(sk_self)
        def _():
            r.skin[x] = r.skpad[...]

        @pl.when(jnp.logical_not(sk_self))
        def _():
            remote(r.skpad, r.skin.at[x], S_SK + x, quad(2 + c)).start()

        own_row = iota((HP, 1), 0)
        live = (own_row < half) & ((own_row + half * x).astype(F32) < length)
        r.dfin[c, hx] = jnp.where(live, mm(spread, r.cot[...]), 0.0).astype(B16)

        for ref in (r.xin, r.normed, r.normed2, r.hidden):
            ref[S:, :] = jnp.zeros((z.SP - S, ref.shape[1]), B16)
        r.heads[...] = jnp.zeros(r.heads.shape, B16)
        for i, ref in enumerate((r.sb, r.g1, r.h1, r.pb, r.g2, r.h2, r.b2)):
            r.rowv[i : i + 1, :] = ref[...].astype(F32).reshape(1, D)
        r.b1v[...] = r.b1[...].astype(F32).reshape(1, z.FF)

        for h in range(2):
            @pl.when((c == 0) & jnp.logical_not(tok_self & (h == 0)))
            def _(h=h):
                wait_recv(r.tokin.at[h], S_TOK + h)

            @pl.when((c == 1) & jnp.logical_not(sk_self & (h == 1)))
            def _(h=h):
                wait_recv(r.skin.at[h], S_SK + h)

        remote(r.dfin.at[c, hx], r.dfin.at[c, hx], S_COT, xpeer).start()
        remote(r.dfin.at[c, hx], r.dfin.at[c, hx], S_COT + 1, peer).start()

        @pl.when(c == 0)
        def _():
            for h in range(2):
                r.xin[h * HP : (h + 1) * HP, :] = r.tokin[h]

        @pl.when(c == 1)
        def _():
            r.xin[0:S, 0 : z.WS] = r.skin[0, :, 0 : z.WS]
            r.xin[0:S, z.WS : z.W] = r.skin[0, :, z.WS : z.W] + r.skin[1, :, 0 : z.W - z.WS]
            r.xin[0:S, z.W : D] = r.skin[1, :, z.W - z.WS : z.W]

        load(r.sw.at[at16(D * c, D)], r.f1v.at[:, 0:D], 0).wait()
        partial_sums(lambda i: mm(r.xin[0:S], r.f1v[:, lanes_of(i)]), r.acc0, r.pin0, S_P0)
        spread_blocks(r.xin, r.sts, z.rs, z.rsp, 0, r.LTs, S_TS, 0)

        @pl.when(jnp.logical_not(tok_self))
        def _():
            wait_send(r.tokpad, S_TOK + x)

        @pl.when(jnp.logical_not(sk_self))
        def _():
            wait_send(r.skpad, S_SK + x)

    def ff_loads():
        return [load(r.f1.at[:, at128(z.FH * c, z.FH)], r.f1v, 5), load(r.f2.at[at16(z.FH * c, z.FH), :], r.f2v, 6)]

    def forward():
        scoped(scope_start(z), begin)
        for v in ff_loads():
            v.start(priority=1)
        partial_done(r.pin0, S_P0)

        def norm_one(i):
            at = rows_of(i)
            v = r.acc0[at] + whole(r.pin0, at) + rowp(SB)
            r.acc0[at] = v
            r.normed[at] = normalise(v, rowp(G1), rowp(H1)).astype(B16)

        loop(S // ROWS, norm_one, S // ROWS)
        for v in qkv_loads(r.qwv):
            v.wait()

        def qkv_tile(i):
            r.pk[:, lanes_of(i)] = mm(r.normed[0:S], r.qwv[:, lanes_of(i)]).astype(B16)

        loop(3 * z.W // TILE, qkv_tile)

        wait_recv(r.dfin.at[c, hx1], S_COT)
        remote(r.dfin.at[c, hx1], r.dfin.at[c, hx1], S_COT + 2, peer).start()

        wait_recv(r.lent.at[1], S_LEN)
        slot_col = iota((1, S), 1)
        slot_of = jnp.where(slot_col < HP, slot_col, slot_col - (HP - half))
        key_ok = ((slot_col < half) | ((slot_col >= HP) & (slot_col < HP + half))) & (
            slot_of.astype(F32) < length_here()
        )

        def head_forward(h):
            start, keep = head_window(h)
            query = r.pk[:, pl.ds(start, span)] * keep.astype(B16)
            key = r.pk[:, at128(z.W + start, span)]
            value = r.pk[:, at128(2 * z.W + start, span)]
            scores = jnp.where(key_ok, mm_nt(query, key) * scale, MASKED)
            top = jnp.max(scores, axis=-1, keepdims=True)
            e = jnp.exp(scores - top)
            probs = (e * (1.0 / jnp.sum(e, axis=-1, keepdims=True))).astype(B16)
            r.probs[h] = probs
            at = pl.ds(start, span)
            r.heads[0:S, at] = r.heads[0:S, at] + (mm(probs, value) * keep).astype(B16)

        loop(z.HN, head_forward, 2)

        proj_load(r.pwv).wait()
        partial_sums(lambda i: mm(r.heads[0:S], r.pwv[:, lanes_of(i)]), r.acc1, r.pin1, S_P1)
        whole_blocks(r.normed, r.stq, r.LTq, S_XQ, 1)
        partial_done(r.pin1, S_P1)

        def norm_two(i):
            at = rows_of(i)
            v = r.acc0[at] + r.acc1[at] + whole(r.pin1, at) + rowp(PB)
            r.acc1[at] = v
            r.normed2[at] = normalise(v, rowp(G2), rowp(H2)).astype(B16)

        loop(S // ROWS, norm_two, S // ROWS)

        whole_blocks(r.normed2, r.st1, r.LT1, S_X1, 4)
        wait_recv(r.dfin.at[1 - c, hx], S_COT + 1)
        wait_recv(r.dfin.at[1 - c, hx1], S_COT + 2)
        for v in ff_loads():
            v.wait()

        def hidden_tile(i):
            at = lanes_of(i)
            a = mm(r.normed2[0:S], r.f1v[:, at]) + r.b1v[:, at128(z.FH * c + i * TILE, TILE)]
            dh = mm_nt(r.dfin[x], r.f2v[rows_of(i, TILE), :])
            cdf = 0.5 * (1.0 + lax.erf(a * (2.0**-0.5)))
            pdf = jnp.exp(-0.5 * a * a) * (0.5 / jnp.pi) ** 0.5
            r.hidden[0:S, at] = (a * cdf).astype(B16)
            da = dh * (cdf + a * pdf)
            r.dact[:, at] = da.astype(B16)
            r.fbias[:, at] = fold(da)

        tiles, fq = z.FH // TILE // 2, z.FH // 2
        loop(tiles, lambda i: hidden_tile(tiles * (1 - x) + i), tiles)
        remote(r.dact.at[:, at128(fq * (1 - x), fq)], r.R1.at[x], S_R1, xpeer).start()
        relay(r.LTq, c, S_XQ)
        relay(r.LT1, c, S_X1)
        loop(tiles, lambda i: hidden_tile(tiles * x + i), tiles)
        partial_sums(lambda i: mm_nt(r.dact[...], r.f1v[rows_of(i, TILE), :]), r.acc2, r.pin0, S_P2)
        spread_blocks(r.hidden, r.st2, z.r2, z.r2p, 0, r.LT2, S_T2, 8)
        local(r.dact.at[:, at128(fq * x, fq)], r.R1.at[x], 3).start(priority=1)

        def result_tile(i):
            at = lanes_of(i)
            r.atile[...] = mm(r.hidden[0:S], r.f2v[:, at])
            r.acc3[:, at] = r.atile[hc]
            r.tokin[0, :, at] = r.atile[hc1].astype(B16)

        loop(nt, result_tile)
        remote(r.tokin.at[0], r.pin3, S_P3, peer).start()
        spread_sent(r.sts, r.LTs, S_TS, 0)
        wait_send(r.stq.at[c], S_XQ)
        local(r.stq, r.LTq.at[x], 1).wait()

    def ref(kind, j):
        return getattr(r, kind + j.name)

    def tile(j, i):
        return at128(j.start + i * j.w, j.w)

    def group_loads(j, part):
        n = GROUPS.index(j.group)
        s = n % r.slotl.shape[0]
        left = getattr(r, "LT" + j.group)
        right = {"2": r.dfin, "1": r.R1, "p": r.Rp, "q": r.Rq, "s": r.dbase}[j.group]
        some = slice(0, 2) if part is None else slice(part, part + 1)
        for i in range(2):
            yield pltpu.make_async_copy(
                left.at[i, :, some], r.slotl.at[s, i, :, some, :, 0 : j.rp], r.semld.at[n, 2 * (part or 0) + i]
            )
            if not part:
                yield pltpu.make_async_copy(
                    right.at[i], r.slotr.at[s, i * z.SP : i * z.SP + S, 0 : right.shape[-1]], r.semld.at[n, 4 + i]
                )

    def kept(j, s, keep, part=None):
        at = [slice(None)] * z.bits
        for b in j.order[:s]:
            at[z.bits - 1 - b] = bit[b]
        b = j.order[s]
        at[z.bits - 1 - b] = bit[b] if keep else 1 - bit[b]
        if part is not None:
            at[1] = slice(part, part + 1)
        return tuple(at)

    def landed(j, s):
        return getattr(r, f"rv{j.name}{s}")

    def half_copy(j, s, i, part=0):
        split = s == 0 and j.parts > 1
        src = ref("pr", j).at[(i, *kept(j, s, False, part if split else None))]
        dst = landed(j, s)
        lead = (i, slice(None), slice(part, part + 1)) if split else (i,)
        n = j.base + part * j.nt + i
        return copy_to(src, dst.at[lead], r.semgs.at[s, n], r.semgr.at[s, n], across[j.order[s]])

    def prep(j, part=None):
        for v in group_loads(j, part):
            v.start(priority=1)

    def ready(j, part=None):
        for v in group_loads(j, part):
            v.wait()

    def products(j, part=0):
        s = GROUPS.index(j.group) % r.slotl.shape[0]

        def step(i):
            at = tile(j, i)
            if j.parts > 1:
                left = [r.slotl[s, n, :, part, :, 0 : j.rp] for n in range(2)]
                to = (slice(None), part)
            else:
                left = [r.slotl[s, n, :, :, :, 0 : j.rp] for n in range(2)]
                to = ()
            left = [v.reshape(z.QN // j.parts * j.rp, z.SP) for v in left]
            out = mm(jnp.concatenate(left, axis=1), r.slotr[s, :, at])
            shape = (2,) * (z.bits - (j.parts > 1)) + (j.rp, j.w)
            ref("pr", j)[(i, *to)] = out.astype(B16).reshape(shape)
            half_copy(j, 0, i, part).start()

        loop(j.nt, step)

    def sums(j, s, store=None):
        def step(i):
            at = tile(j, i)
            for part in range(j.parts if s == 0 else 1):
                half_copy(j, s, i, part).wait_recv()
            here = (i, *kept(j, s, True))
            theirs = landed(j, s)
            if z.far and s > 0:
                n = 2 ** (z.bits - 1 - s)
                stage = r.zin.at[0:n, 0 : j.rp, 0 : j.w]
                for k in range(n):
                    pick = tuple(k // 2**b % 2 for b in reversed(range(z.bits - 1 - s)))
                    fetch = local(theirs.at[(i, *pick)], stage.at[k], 15)
                    fetch.start()
                    fetch.wait()
                piece = stage[...].reshape(theirs.shape[1:])
            else:
                piece = theirs[i]
            total = ref("pr", j)[here].astype(F32) + piece.astype(F32)
            if s < z.bits - 1:
                ref("pr", j)[here] = total.astype(B16)
                half_copy(j, s + 1, i).start()
            else:
                store(at, total)

        loop(j.nt, step)

    def more_sums(j):
        for s in range(2, z.bits - 1):
            sums(j, s)

    def sums_sent(j):
        def step(i):
            for s in range(z.bits):
                for part in range(j.parts if s == 0 else 1):
                    half_copy(j, s, i, part).wait_send()

        loop(j.nt, step)

    rq = z.r1 // 4

    def fix_copy(n, g, t):
        k = lax.rem(me + t, 4)
        src, dst = getattr(r, "fs" + g), getattr(r, "fr" + g)
        return copy_to(src.at[k], dst.at[me], r.semfs.at[n, t - 1], r.semfr.at[n, t - 1], quad(k))

    def fix_start(n, g):
        for t in range(1, 4):
            fix_copy(n, g, t).start()
        getattr(r, "fr" + g)[me] = getattr(r, "fs" + g)[me]

    def fix_wait(n, g):
        for t in range(1, 4):
            fix_copy(n, g, t).wait()

    def direct(out):
        def store(at, total):
            out[:, at] = total[0 : out.shape[0]]

        return store

    def summed(out):
        def store(at, total):
            w = total.shape[1]
            r.sumt[:, 0:w] = total
            for k in range(4):
                out[k, 0:rq, at] = r.sumt[k * rq : (k + 1) * rq, 0:w]

        return store

    v_devs = (peer, xpeer, *across)

    def v_copy(s):
        return copy_to(r.vb.at[s], r.vr.at[s], r.semvs.at[s], r.semvr.at[s], v_devs[s])

    def v_step(s):
        if s > 0:
            v_copy(s - 1).wait()
            r.vb[s] = r.vb[s - 1] + r.vr[s - 1]
        if s < len(v_devs):
            v_copy(s).start()

    def back():
        for v in qkv_loads(r.qwb):
            v.start(priority=1)
        proj_load(r.pwb).start(priority=1)
        for s in range(r.slotr.shape[0]):
            for i in range(2):
                r.slotr[s, i * z.SP + S : (i + 1) * z.SP, :] = jnp.zeros((z.SP - S, D), B16)
        r.dpack[...] = jnp.zeros(r.dpack.shape, B16)
        partial_done(r.pin0, S_P2)

        def norm_two_back(i, sums):
            at = rows_of(i)
            dn = r.acc2[at] + whole(r.pin0, at)
            dv, dg = norm_back(r.acc1[at], dn, rowp(G2))
            df = r.dfin[x, at].astype(F32)
            dm = df + dv
            r.acc2[at] = dm
            r.dmidl[at] = dm.astype(B16)
            return sums[0] + fold(dg), sums[1] + fold(dn), sums[2] + fold(df), sums[3] + fold(dm)

        dg2, dh2, db2, dpb = lax.fori_loop(0, S // ROWS, norm_two_back, (zero, zero, zero, zero))
        local(r.dmidl, r.Rp.at[x], 6).start(priority=1)
        wait_recv(r.LT1.at[1 - x, 1 - c], S_X1 + 1)
        local(r.st1, r.LT1.at[x], 4).wait()
        wait_recv(r.R1.at[1 - x], S_R1)
        local(r.R1.at[x], r.R1.at[x], 3).wait()
        prep(j1a)
        r.vb[0] = jnp.zeros((16, D), F32)
        first = jnp.where(c == 0, 1.0, 0.0)
        for i, v in ((3, dpb), (4, dg2), (5, dh2), (6, db2)):
            r.vb[0, i : i + 1, :] = v * first
        for j in range(z.FH // D):
            v = r.fbias[:, j * D : (j + 1) * D]
            r.vb[0, 8 + j : 9 + j, :] = v * first
            r.vb[0, 10 + j : 11 + j, :] = v * (1.0 - first)

        proj_load(r.pwb).wait()
        r.skin[0] = mm_nt(r.dmidl[...], r.pwb[...]).astype(B16)
        ready(j1a)
        products(j1a)
        products(j1b)

        def head_backward(h):
            start, keep = head_window(h)
            low = keep.astype(B16)
            at_q, at_k, at_v = pl.ds(start, span), at128(z.W + start, span), at128(2 * z.W + start, span)
            query, key, value = r.pk[:, at_q], r.pk[:, at_k], r.pk[:, at_v]
            dh = r.skin[0, :, at_q]
            probs = r.probs[h]
            dp = mm_nt(dh * low, value)
            pf = probs.astype(F32)
            delta = jnp.sum(dp * pf, axis=-1, keepdims=True)
            ds = (pf * (dp - delta) * scale).astype(B16)
            r.dpack[:, at_q] = r.dpack[:, at_q] + (mm(ds, key) * keep).astype(B16)
            r.dpack[:, at_k] = r.dpack[:, at_k] + (mm_tn(ds, query) * keep).astype(B16)
            r.dpack[:, at_v] = r.dpack[:, at_v] + (mm_tn(probs, dh) * keep).astype(B16)

        def slab_of(mine, part):
            first = z.LO * c + (z.HS - z.SW) * part
            row, lane = iota((z.SL, z.SL), 0), iota((z.SL, z.SL), 1)
            out = []
            for t in range(3):
                to = z.HS * t // LANE * LANE
                move = onehot((row - first == lane - (z.HS * t - to)) & (row >= first) & (row < first + z.HS))
                out.append((to, mm(r.dpack[:, at128(z.W * t + z.SW * part, z.SL)], move).astype(B16)))
            for at in range(0, z.PQ, LANE):
                held = [v[:, at - to : at - to + LANE] for to, v in out if to <= at < to + z.SL]
                r.slab[mine, :, at : at + LANE] = held[0] if len(held) == 1 else held[0] + held[1]

        nh = z.HN // 2
        loop(nh, lambda i: head_backward(nh * (1 - x) + i), 2)
        slab_of(0, 1 - x)
        remote(r.slab.at[0], r.Rq.at[x], S_RQ, xpeer).start()
        remote(r.dmidl.at[hc], r.Rp.at[x, hc], S_XP, xpeer).start()
        block_out()
        spread_here(r.LT2, S_T2)
        local(r.st2.at[0], r.LT2.at[x, 0], 8).wait()
        prep(j2a)
        ready(j2a)
        products(j2a)
        products(j2b)
        loop(nh, lambda i: head_backward(nh * x + i), 2)
        for v in qkv_loads(r.qwb):
            v.wait()
        partial_sums(lambda i: mm_nt(r.dpack[...], r.qwb[rows_of(i, TILE), :]), r.acc1, r.pin1, S_P4)
        slab_of(1, x)
        local(r.slab.at[1], r.Rq.at[x], 7).start(priority=1)
        spread_blocks(r.heads, r.stp, z.rp, z.rpp, z.LO * c, r.LTp, S_TP, 2)
        sums(j1a, 0)
        sums(j1b, 0)
        relay(r.Rp, hc, S_XP)

    def block_out():
        wait_recv(r.pin3, S_P3)
        slot_row = iota((HP, 1), 0)
        out_ok = (slot_row < half) & ((slot_row + half * c).astype(F32) < length_here())
        total = r.acc1[hc] + r.acc3[...] + r.pin3[...].astype(F32) + rowp(B2)
        r.tokin[1] = jnp.where(out_ok, total, 0.0).astype(B16)

        @pl.when(c == x)
        def _():
            r.bosum[...] = r.tokin[1]

    def finish():
        weight = [
            load(r.sw.at[0:D], r.swb, 8),
            load(r.sw.at[at16(D + z.DH * x, z.DH)], r.swb.at[0 : z.DH], 9),
        ]
        weight[0].start(priority=1)
        partial_done(r.pin1, S_P4)

        def norm_one_back(i, sums):
            at = rows_of(i)
            dn = r.acc1[at] + whole(r.pin1, at)
            dv, dg = norm_back(r.acc0[at], dn, rowp(G1))
            db = r.acc2[at] + dv
            r.dbase[x, at] = db.astype(B16)
            return sums[0] + fold(dg), sums[1] + fold(dn), sums[2] + fold(db)

        dg1, dh1, dsb = lax.fori_loop(0, S // ROWS, norm_one_back, (zero, zero, zero))
        first = jnp.where(c == 0, 1.0, 0.0)
        for i, v in enumerate((dsb, dg1, dh1)):
            r.vb[0, i : i + 1, :] = v * first
        v_step(0)

        remote(r.dbase.at[x, hc], r.dbase.at[x, hc], S_XS, xpeer).start()
        wait_recv(r.LTq.at[1 - x, 1 - c], S_XQ + 1)
        wait_recv(r.Rq.at[1 - x], S_RQ)
        local(r.Rq.at[x], r.Rq.at[x], 7).wait()
        prep(jqa)
        ready(jqa)
        products(jqa)
        products(jqb)
        wait_recv(r.Rp.at[1 - x, hc1], S_XP + 1)
        local(r.dmidl, r.Rp.at[x], 6).wait()
        spread_here(r.LTp, S_TP)
        spread_sent(r.stp, r.LTp, S_TP, 2)
        prep(jp)
        v_step(1)
        sums(j2b, 0)
        sums(j1b, 1)
        ready(jp)
        products(jp)
        sums(j1a, 1)
        relay(r.dbase, hc, S_XS)
        spread_here(r.LTs, S_TS)
        sums(j2a, 0)
        wait_recv(r.dbase.at[1 - x, hc1], S_XS + 1)
        prep(js)
        v_step(2)

        @pl.when(c != x)
        def _():
            remote(r.tokin.at[1], r.bosum, S_BO, (2 * q + x, c)).start()

        ready(js)
        products(js)
        more_sums(j1a)
        more_sums(j1b)
        v_step(3)
        sums(j2b, 1)
        sums(jp, 0)
        sums(jqb, 0)
        sums(j1b, z.bits - 1, summed(r.fs1))
        weight[0].wait()
        r.tg[...] = mm_nt(r.dbase[c, hx], r.swb[...]).astype(B16)[0:half]
        weight[1].start(priority=1)
        v_step(4)
        sums(j1a, z.bits - 1, summed(r.fs1))
        fix_start(0, "1")
        sums(j2a, 1)
        sums(jqa, 0)
        more_sums(j2a)
        more_sums(j2b)
        sums(j2b, z.bits - 1, direct(r.w2))
        weight[1].wait()
        sg = mm_nt(r.dbase[c], r.swb[0 : z.DH, :]).astype(B16)
        row, col = iota((2 * half, S), 0), iota((2 * half, S), 1)
        back_rows = onehot(((row < half) & (row == col)) | ((row >= half) & (col == row + (HP - half))))
        r.sg[...] = mm(back_rows, sg).astype(B16)
        for s in range(5, len(v_devs) + 1):
            v_step(s)
        r.vout[...] = r.vb[len(v_devs)]
        sums(jqb, 1)
        more_sums(jqb)
        sums(jp, 1)
        more_sums(jp)
        sums(js, 0)
        sums(j2a, z.bits - 1, direct(r.w2))

        @pl.when(c == x)
        def _():
            r.bosum[...] = r.tokin[1]

        @pl.when(c != x)
        def _():
            remote(r.tokin.at[1], r.bosum, S_BO, (2 * q + x, c)).wait()

        r.bo[...] = r.bosum[0:half]
        sums(jqa, 1)
        more_sums(jqa)
        sums(jqb, z.bits - 1, summed(r.fsq))
        fix_wait(0, "1")
        for k in range(4):
            r.w1[:, k * (z.FH // 2) : (k + 1) * (z.FH // 2)] = r.fr1[k, 0:rq]
        sums(jp, z.bits - 1, direct(r.wp))
        sums(js, 1)
        more_sums(js)
        sums(jqa, z.bits - 1, summed(r.fsq))
        fix_start(1, "q")
        sums(js, z.bits - 1, direct(r.ws))
        fix_wait(1, "q")
        for t in range(3):
            r.wq[:, t * D : (t + 1) * D] = jnp.concatenate(
                [r.frq[k, 0:rq, t * z.HS : (t + 1) * z.HS] for k in range(4)], axis=1
            )

        wait_send(r.lent.at[0], S_LEN)
        for j in range(3):
            wait_send(r.dfin.at[c, hx], S_COT + j)
        for j in range(3):
            wait_send(r.st2.at[0], S_T2 + j)
        wait_send(r.tokin.at[0], S_P3)
        wait_send(r.st1.at[c], S_X1)
        wait_send(r.dmidl.at[hc], S_XP)
        wait_send(r.dbase.at[x, hc], S_XS)
        wait_send(r.LTq.at[1 - x, c], S_XQ + 1)
        wait_send(r.LT1.at[1 - x, c], S_X1 + 1)
        wait_send(r.Rp.at[1 - x, hc], S_XP + 1)
        wait_send(r.dbase.at[1 - x, hc], S_XS + 1)
        wait_send(r.R1.at[x], S_R1)
        wait_send(r.slab.at[0], S_RQ)
        for j in jobs:
            sums_sent(j)

    def backward():
        scoped(scope_back(z), back)
        scoped(scope_end(z), finish)

    scoped(scope_one(z), forward)
    scoped(scope_two(z), backward)


def call(z, *args):
    outs = out_shapes(z)
    anywhere, vmem = pl.BlockSpec(memory_space=pl.ANY), pl.BlockSpec(memory_space=pltpu.VMEM)
    names = (*any_outs(z), *VMEM_OUTS)
    res = pl.pallas_call(
        functools.partial(kernel, z),
        out_shape=[outs[n] for n in names],
        in_specs=[pl.BlockSpec(memory_space=pltpu.SMEM), *([vmem] * 11), *([anywhere] * 5)],
        out_specs=[anywhere] * len(any_outs(z)) + [vmem] * len(VMEM_OUTS),
        scratch_shapes=list(scratch_of(z).values()),
        compiler_params=pltpu.CompilerParams(
            collective_id=0, has_side_effects=True, vmem_limit_bytes=VMEM_BYTES
        ),
        name="block",
    )(*args)
    return dict(zip(names, res))


def shards(tokens, skip_feats, lengths, cotangent, skip_weight, skip_bias, norm1_gain, norm1_bias, qkv_weight,
           proj_weight, proj_bias, norm2_gain, norm2_bias, fc1_weight, fc1_bias, fc2_weight, fc2_bias):
    dp_count = lax.axis_size("dp")
    half, width = tokens.shape[1:]
    z = sizes(half, width, fc1_weight.shape[1], dp_count)
    g = call(z, lengths, tokens[0], skip_feats[0], cotangent[0], skip_bias, norm1_gain, norm1_bias, proj_bias,
             norm2_gain, norm2_bias, fc1_bias, fc2_bias, skip_weight, qkv_weight, proj_weight, fc1_weight, fc2_weight)
    vec = g["vout"]
    b = 2 * lax.axis_index("dp") + lax.axis_index("seq")
    own = lax.dynamic_slice(vec, (0, b * z.rp), (8, z.rp))
    fb = lax.dynamic_slice(vec[8 : 8 + z.FF // width].reshape(-1), (b * z.r2,), (z.r2,))
    return (g["bo"][None], g["tg"][None], g["sg"][None], g["ws"], own[0], own[1], own[2], g["wq"], g["wp"], own[3],
            own[4], own[5], g["w1"], fb, g["w2"], own[6])


def solution(mesh):
    placed = (P("dp", "seq", None), P("dp", None, "seq"), P("dp"), P("dp", "seq", None), *([P()] * 13))
    both = ("dp", "seq")
    return jax.shard_map(
        shards, mesh=mesh, in_specs=placed,
        out_specs=(P("dp", "seq", None), P("dp", "seq", None), P("dp", None, "seq"), P(both, None), P(both), P(both),
                   P(both), P(both, None), P(both, None), P(both), P(both), P(both), P(both, None), P(both),
                   P(both, None), P(both)),
        check_vma=False,
    )
```

time: 1020 us -> 218 us (0.21)
  blocking collectives: 545 us -> 0 us
  Pallas kernels: 0 us -> 205 us
  local copies, waits for them, and re-layouts: 169 us -> 11.1 us
  matrix products: 151 us -> 0 us
  starting transfers between devices: 53.9 us -> 0 us
  waiting for transfers between devices: 52.6 us -> 0 us
  other arithmetic: 23.7 us -> 0 us
  between operations: 17.7 us -> 1.35 us
    unnamed x2 -> x0, blocking collectives: 357 us -> none
    pallas_call x0 -> x1, Pallas kernels: none -> 205 us  [call(): pl.pallas_call(functools.partial(kernel, z), out_shape=[outs[n] for n in...]
    all_gather x8 -> x0, blocking collectives: 189 us -> none  [the longest x1 34.5 us: shards(): lax.all_gather(d_middle_low, 'seq', axis=1, tiled=True)]
    dot_general x20 -> x0, matrix products: 146 us -> none  [matmul(): return jnp.einsum(form, left, right, preferred_element_type=jnp.float32)]
    unnamed x123 -> x20, local copies, waits for them, and re-layouts: 83 us -> 8.3 us
    unnamed x12 -> x0, starting transfers between devices: 46 us -> none
    unnamed x19 -> x0, waiting for transfers between devices: 25.6 us -> none
    all_gather x4 -> x0, waiting for transfers between devices: 23.8 us -> none  [the longest x1 23.8 us: shards(): lax.all_gather(joined, 'seq', axis=1, tiled=True)]
  transfers between devices with their start and end apart: 19 -> 0, of which waited for: 3 -> 0; matrix products, arithmetic and copies ran while one was open for 52% -> 0% of each run, Pallas kernels for 0% -> 0%
where the time goes in v1:
time: 218 us
  Pallas kernels  205 us (94%)
  local copies, waits for them, and re-layouts  11.1 us (5%)
    pallas_call x1, Pallas kernels, call(): pl.pallas_call(functools.partial(kernel, z), out_shape=[outs[n] for n in...  205 us
    unnamed x20, local copies, waits for them, and re-layouts  8.3 us

profile of v1, /device:TPU:0, one launch (start us, length us, event | category | flops | bytes accessed | tf_op | source)
XLA Modules:
  0.0 217.9 jit_solution(6576867229705935794)
XLA Ops:
  1.3 205.4 %block.1 = (bf16[2,2,2,2,144,384]{5,4,3,2,1,0:T(8,128)(2,1)}, bf16[2,2,2,2,144,384]{5,4,3,2,1,0:T(8,128)(2,1)}, bf16[2,2,2,2,144,384]{5,4,3,2,1,0:T(8,128)(2,1)}...) custom-call(s32[1]{0:T(128)S(6)} %copy.41.refs_0_, ...), custom_call_target="tpu_custom_call" | custom-call | tf_op jit(solution)/shard_map/block/pallas_call | solution.py:1032
  206.7 0.0 copy-start.3
  206.8 0.0 copy-start.4
  206.8 0.0 copy-start.2
  206.8 0.9 constant_dynamic-slice_fusion
  207.7 0.5 slice_bitcast_fusion
  208.2 0.8 slice.30
  209.0 0.6 dynamic_slice.7
  209.6 1.8 copy.42
  211.4 0.0 copy-start.5
  211.4 0.0 copy-start
  211.4 1.8 copy.43
  213.2 0.0 copy-done.3
  213.2 0.8 copy.44
  214.0 0.0 copy-done.4
  214.0 0.7 copy.45
  214.7 0.0 copy-done.2
  214.7 0.8 copy.46
  215.5 0.0 copy-done.5
  215.5 0.7 copy.47
  216.2 0.0 copy-done
  216.2 0.9 copy.48
  217.1 0.0 copy-done.1
  217.1 0.8 copy.49
  (2 shorter events, 0.0 us)
Async XLA Ops:
  206.7 6.5 %copy-start.3 = (bf16[322,576]{1,0:T(8,128)(2,1)S(1)}, bf16[322,576]{1,0:T(8,128)(2,1)}, u32[]{:S(2)}) copy-start(bf16[322,576]{1,0:T(8,128)(2,1)} %get-tuple-element.27) | copy-start | bytes 1112836
  206.8 7.2 %copy-start.4 = (f32[72,1152]{1,0:T(8,128)S(1)}, f32[72,1152]{1,0:T(8,128)}, u32[]{:S(2)}) copy-start(f32[72,1152]{1,0:T(8,128)} %get-tuple-element.60) | copy-start | bytes 995332
  206.8 8.0 %copy-start.2 = (f32[36,3456]{1,0:T(8,128)S(1)}, f32[36,3456]{1,0:T(8,128)}, u32[]{:S(2)}) copy-start(f32[36,3456]{1,0:T(8,128)} %get-tuple-element.64) | copy-start | bytes 1492996
  211.4 4.1 %copy-start.5 = (f32[36,1152]{1,0:T(8,128)S(1)}, f32[36,1152]{1,0:T(8,128)}, u32[]{:S(2)}) copy-start(f32[36,1152]{1,0:T(8,128)} %get-tuple-element.65) | copy-start | bytes 497668
  211.4 4.8 %copy-start = (f32[36,4608]{1,0:T(8,128)S(1)}, f32[36,4608]{1,0:T(8,128)}, u32[]{:S(2)}) copy-start(f32[36,4608]{1,0:T(8,128)} %get-tuple-element.69) | copy-start | bytes 1990660
  214.0 3.1 %copy-start.1 = (f32[144,1152]{1,0:T(8,128)S(1)}, f32[144,1152]{1,0:T(8,128)}, u32[]{:S(2)}) copy-start(f32[144,1152]{1,0:T(8,128)} %get-tuple-element.71) | copy-start | bytes 1990660

commit v2 on v1

--- a/solution.py
+++ b/solution.py
@@ -123,7 +123,7 @@
 
 def landing_of(z):
     return {
-        f"rv{j.name}{s}": ((j.nt,) + (2,) * (z.bits - 1 - s) + (j.rp, j.w), z.far and s > 0)
+        f"rv{j.name}{s}": ((j.nt,) + (2,) * (z.bits - 1 - s) + (j.rp, j.w), z.far)
         for j in jobs_of(z)[0]
         for s in range(z.bits)
     }
@@ -139,7 +139,7 @@
     return LEFT_OUTS + tuple(n for n, (_, out) in landing_of(z).items() if out)
 
 
-VMEM_OUTS = ("bo", "tg", "sg", "w2", "w1", "wp", "wq", "ws", "vout")
+VMEM_OUTS = ("bo", "tg", "sg", "w2", "fr1", "wp", "frq", "ws", "vout")
 
 
 def out_shapes(z):
@@ -159,9 +159,9 @@
         tg=s((z.half, z.D), B16),
         sg=s((2 * z.half, z.DH), B16),
         w2=s((z.r2, z.D), F32),
-        w1=s((z.r1 // 4, z.FF), F32),
+        fr1=s((4, up(z.r1 // 4, 8), z.FH // 2), F32),
         wp=s((z.rp, z.D), F32),
-        wq=s((z.r1 // 4, 3 * z.D), F32),
+        frq=s((4, up(z.r1 // 4, 8), z.PQ), F32),
         ws=s((z.rs, z.D), F32),
         vout=s((16, z.D), F32),
     )
@@ -170,7 +170,6 @@
 def scratch_of(z):
     v, dma = pltpu.VMEM, pltpu.SemaphoreType.DMA
     jobs, tiles = jobs_of(z)
-    fp = up(z.r1 // 4, 8)
     out = dict(
         tokin=v((2, z.HP, z.D), B16),
         skin=v((2, z.S, z.W), B16),
@@ -201,8 +200,6 @@
     for n, (shape, outside) in landing_of(z).items():
         if not outside:
             out[n] = v(shape, B16)
-    for n, cols in (("1", z.FH // 2), ("q", z.PQ)):
-        out["fr" + n] = v((4, fp, cols), F32)
     out["wsem"] = dma((12,))
     out["lsem"] = dma((16,))
     out["ssem"], out["rsem"] = dma((64,)), dma((64,))
@@ -250,7 +247,7 @@
         slotr=v((1, 2 * z.SP, z.D), B16),
     )
     if z.far:
-        out["zin"] = v((z.QP, max(j.rp for j in jobs), 512), B16)
+        out["zin"] = v((2 * z.QP, max(j.rp for j in jobs), 512), B16)
     for j in jobs:
         out["pr" + j.name] = v((j.nt,) + (2,) * z.bits + (j.rp, j.w), B16)
     return out
@@ -707,7 +704,7 @@
                 half_copy(j, s, i, part).wait_recv()
             here = (i, *kept(j, s, True))
             theirs = landed(j, s)
-            if z.far and s > 0:
+            if z.far:
                 n = 2 ** (z.bits - 1 - s)
                 stage = r.zin.at[0:n, 0 : j.rp, 0 : j.w]
                 for k in range(n):
@@ -802,7 +799,7 @@
             r.dmidl[at] = dm.astype(B16)
             return sums[0] + fold(dg), sums[1] + fold(dn), sums[2] + fold(df), sums[3] + fold(dm)
 
-        dg2, dh2, db2, dpb = lax.fori_loop(0, S // ROWS, norm_two_back, (zero, zero, zero, zero))
+        dg2, dh2, db2, dpb = lax.fori_loop(0, S // ROWS, norm_two_back, (zero, zero, zero, zero), unroll=S // ROWS)
         local(r.dmidl, r.Rp.at[x], 6).start(priority=1)
         wait_recv(r.LT1.at[1 - x, 1 - c], S_X1 + 1)
         local(r.st1, r.LT1.at[x], 4).wait()
@@ -901,7 +898,7 @@
             r.dbase[x, at] = db.astype(B16)
             return sums[0] + fold(dg), sums[1] + fold(dn), sums[2] + fold(db)
 
-        dg1, dh1, dsb = lax.fori_loop(0, S // ROWS, norm_one_back, (zero, zero, zero))
+        dg1, dh1, dsb = lax.fori_loop(0, S // ROWS, norm_one_back, (zero, zero, zero), unroll=S // ROWS)
         first = jnp.where(c == 0, 1.0, 0.0)
         for i, v in enumerate((dsb, dg1, dh1)):
             r.vb[0, i : i + 1, :] = v * first
@@ -985,8 +982,6 @@
         more_sums(jqa)
         sums(jqb, z.bits - 1, summed(r.fsq))
         fix_wait(0, "1")
-        for k in range(4):
-            r.w1[:, k * (z.FH // 2) : (k + 1) * (z.FH // 2)] = r.fr1[k, 0:rq]
         sums(jp, z.bits - 1, direct(r.wp))
         sums(js, 1)
         more_sums(js)
@@ -994,10 +989,6 @@
         fix_start(1, "q")
         sums(js, z.bits - 1, direct(r.ws))
         fix_wait(1, "q")
-        for t in range(3):
-            r.wq[:, t * D : (t + 1) * D] = jnp.concatenate(
-                [r.frq[k, 0:rq, t * z.HS : (t + 1) * z.HS] for k in range(4)], axis=1
-            )
 
         wait_send(r.lent.at[0], S_LEN)
         for j in range(3):
@@ -1043,6 +1034,53 @@
     return dict(zip(names, res))
 
 
+def place(z, bo, tg, sg, w2, fr1, wp, frq, ws, vout, *outs):
+    (bo_o, tg_o, sg_o, ws_o, sb_o, g1_o, h1_o, wq_o, wp_o, pb_o, g2_o, h2_o, w1_o, b1_o, w2_o, b2_o) = outs
+    for src, dst in ((bo, bo_o), (tg, tg_o), (sg, sg_o), (ws, ws_o), (wp, wp_o), (w2, w2_o)):
+        dst[...] = src[...]
+    rq, fq = z.r1 // 4, z.FH // 2
+    for k in range(4):
+        w1_o[:, k * fq : (k + 1) * fq] = fr1[k, 0:rq]
+    for t in range(3):
+        wq_o[:, t * z.D : (t + 1) * z.D] = jnp.concatenate(
+            [frq[k, 0:rq, t * z.HS : (t + 1) * z.HS] for k in range(4)], axis=1
+        )
+    block = 2 * lax.axis_index("dp") + lax.axis_index("seq")
+
+    def take(v, first, n):
+        pick = jnp.where(iota((z.D, n), 0) == iota((z.D, n), 1) + first, 1.0, 0.0)
+        return lax.dot_general(
+            v, pick, (((1,), (0,)), ((), ())), preferred_element_type=F32, precision=lax.Precision.HIGHEST
+        )
+
+    own = take(vout[0:8], block * z.rp, z.rp)
+    for i, dst in enumerate((sb_o, g1_o, h1_o, pb_o, g2_o, h2_o, b2_o)):
+        dst[...] = own[i : i + 1, :].reshape(z.rp)
+    per = z.D // z.r2
+    row = iota((8, z.D), 0)
+    held = jnp.where(row == block // per, vout[8:16], 0.0)
+    b1_o[...] = jnp.sum(take(held, lax.rem(block, per) * z.r2, z.r2), axis=0, keepdims=True).reshape(z.r2)
+
+
+def call_place(z, g):
+    s = jax.ShapeDtypeStruct
+    one = s((z.rp,), F32)
+    vmem = pl.BlockSpec(memory_space=pltpu.VMEM)
+    res = [
+        s((z.half, z.D), B16), s((z.half, z.D), B16), s((2 * z.half, z.DH), B16), s((z.rs, z.D), F32), one, one, one,
+        s((z.r1 // 4, 3 * z.D), F32), s((z.rp, z.D), F32), one, one, one, s((z.r1 // 4, z.FF), F32), s((z.r2,), F32),
+        s((z.r2, z.D), F32), one,
+    ]
+    return pl.pallas_call(
+        functools.partial(place, z),
+        out_shape=res,
+        in_specs=[vmem] * len(VMEM_OUTS),
+        out_specs=[vmem] * len(res),
+        compiler_params=pltpu.CompilerParams(vmem_limit_bytes=32 * 1024 * 1024),
+        name="place",
+    )(*(g[n] for n in VMEM_OUTS))
+
+
 def shards(tokens, skip_feats, lengths, cotangent, skip_weight, skip_bias, norm1_gain, norm1_bias, qkv_weight,
            proj_weight, proj_bias, norm2_gain, norm2_bias, fc1_weight, fc1_bias, fc2_weight, fc2_bias):
     dp_count = lax.axis_size("dp")
@@ -1050,12 +1088,8 @@
     z = sizes(half, width, fc1_weight.shape[1], dp_count)
     g = call(z, lengths, tokens[0], skip_feats[0], cotangent[0], skip_bias, norm1_gain, norm1_bias, proj_bias,
              norm2_gain, norm2_bias, fc1_bias, fc2_bias, skip_weight, qkv_weight, proj_weight, fc1_weight, fc2_weight)
-    vec = g["vout"]
-    b = 2 * lax.axis_index("dp") + lax.axis_index("seq")
-    own = lax.dynamic_slice(vec, (0, b * z.rp), (8, z.rp))
-    fb = lax.dynamic_slice(vec[8 : 8 + z.FF // width].reshape(-1), (b * z.r2,), (z.r2,))
-    return (g["bo"][None], g["tg"][None], g["sg"][None], g["ws"], own[0], own[1], own[2], g["wq"], g["wp"], own[3],
-            own[4], own[5], g["w1"], fb, g["w2"], own[6])
+    out = call_place(z, g)
+    return (*(v[None] for v in out[:3]), *out[3:])
 
 
 def solution(mesh):

time: 218 us -> 218 us (level)
    pallas_call x0 -> x1, Pallas kernels: none -> 2.75 us  [call_place(): pl.pallas_call(functools.partial(place, z), out_shape=res, in_specs=[vmem...]
    unnamed x20 -> x18, local copies, waits for them, and re-layouts: 8.3 us -> 9.03 us
where the time goes in v2:
time: 218 us; the launch traced here: 217 us
  Pallas kernels  207 us (95%)
  local copies, waits for them, and re-layouts  9.03 us (4%)
    pallas_call x1, Pallas kernels, call(): pl.pallas_call(functools.partial(kernel, z), out_shape=[outs[n] for n in...  204 us
    unnamed x18, local copies, waits for them, and re-layouts  9.03 us

profile of v2, /device:TPU:0, one launch (start us, length us, event | category | flops | bytes accessed | tf_op | source)
XLA Modules:
  0.0 217.0 jit_solution(11451019910390807421)
XLA Ops:
  1.3 203.9 %block.1 = (bf16[2,2,2,2,144,384]{5,4,3,2,1,0:T(8,128)(2,1)}, bf16[2,2,2,2,144,384]{5,4,3,2,1,0:T(8,128)(2,1)}, bf16[2,2,2,2,144,384]{5,4,3,2,1,0:T(8,128)(2,1)}...) custom-call(s32[1]{0:T(128)S(6)} %copy.33.refs_0_, ...), custom_call_target="tpu_custom_call" | custom-call | tf_op jit(solution)/shard_map/block/pallas_call | solution.py:1023
  205.3 0.0 copy-start
  205.3 1.1 copy-done
  206.4 0.0 copy-start.1
  206.4 1.1 copy-done.1
  207.5 0.0 copy-start.2
  207.5 1.1 copy-done.2
  208.5 0.0 copy-start.3
  208.5 1.0 copy-done.3
  209.5 0.0 copy-start.4
  209.5 1.0 copy-done.4
  210.5 0.0 copy-start.5
  210.5 1.0 copy-done.5
  211.5 0.0 copy-start.6
  211.5 1.0 copy-done.6
  212.5 0.0 copy-start.7
  212.5 0.9 copy-done.7
  213.4 0.0 copy-start.8
  213.4 0.9 copy-done.8
  214.3 2.8 %place.1 = (bf16[161,1152]{1,0:T(8,128)(2,1)}, bf16[161,1152]{1,0:T(8,128)(2,1)}, bf16[322,576]{1,0:T(8,128)(2,1)}, f32[72,1152]{1,0:T(8,128)}, f32[36]{0:T(128)...) custom-call(bf16[161,1152]{1,0:T(8,128)(2,1)S(1)} %copy-done.4, ...), custom_call_target="tpu_custom_call" | custom-call | tf_op jit(solution)/shard_map/place/pallas_call | solution.py:1074
Async XLA Ops:
  205.3 1.1 copy-start
  206.4 1.1 copy-start.1
  207.5 1.1 copy-start.2
  208.5 1.0 copy-start.3
  209.5 1.0 copy-start.4
  210.5 1.0 copy-start.5
  211.5 1.0 copy-start.6
  212.5 0.9 copy-start.7
  213.4 0.9 copy-start.8

commit v3 on v2

--- a/solution.py
+++ b/solution.py
@@ -104,7 +104,7 @@
         ("2b", "2", z.r2, z.r2p, 2 * TILE, z.D - 2 * TILE, TILE, 1, far),
         ("1a", "1", z.r1, z.r1p, 0, 2 * TILE, TILE, 1, near),
         ("1b", "1", z.r1, z.r1p, 2 * TILE, z.FH // 2 - 2 * TILE, TILE, 1, far),
-        ("p", "p", z.rp, z.rpp, 0, z.D, TILE, 1, far),
+        ("p", "p", z.rp, z.rpp, 0, z.D, TILE, 1, near),
         ("qa", "q", z.r1, z.r1p, 0, 512, 512, 1, near),
         ("qb", "q", z.r1, z.r1p, 512, z.PQ - 512, TILE, 1, far),
         ("s", "s", z.rs, z.rsp, 0, z.D, TILE, 1, near),
@@ -869,6 +869,10 @@
         spread_blocks(r.heads, r.stp, z.rp, z.rpp, z.LO * c, r.LTp, S_TP, 2)
         sums(j1a, 0)
         sums(j1b, 0)
+        wait_recv(r.LTq.at[1 - x, 1 - c], S_XQ + 1)
+        wait_recv(r.Rq.at[1 - x], S_RQ)
+        local(r.Rq.at[x], r.Rq.at[x], 7).wait()
+        prep(jqa)
         relay(r.Rp, hc, S_XP)
 
     def block_out():
@@ -905,10 +909,6 @@
         v_step(0)
 
         remote(r.dbase.at[x, hc], r.dbase.at[x, hc], S_XS, xpeer).start()
-        wait_recv(r.LTq.at[1 - x, 1 - c], S_XQ + 1)
-        wait_recv(r.Rq.at[1 - x], S_RQ)
-        local(r.Rq.at[x], r.Rq.at[x], 7).wait()
-        prep(jqa)
         ready(jqa)
         products(jqa)
         products(jqb)
@@ -1076,7 +1076,7 @@
         out_shape=res,
         in_specs=[vmem] * len(VMEM_OUTS),
         out_specs=[vmem] * len(res),
-        compiler_params=pltpu.CompilerParams(vmem_limit_bytes=32 * 1024 * 1024),
+        compiler_params=pltpu.CompilerParams(vmem_limit_bytes=VMEM_BYTES),
         name="place",
     )(*(g[n] for n in VMEM_OUTS))
 

time: 218 us -> 210 us (0.963)
  local copies, waits for them, and re-layouts: 9.03 us -> 0 us
    unnamed x18 -> x0, local copies, waits for them, and re-layouts: 9.03 us -> none
where the time goes in v3:
time: 210 us
  Pallas kernels  208 us (99%)
    pallas_call x1, Pallas kernels, call(): pl.pallas_call(functools.partial(kernel, z), out_shape=[outs[n] for n in...  203 us
    pallas_call x1, Pallas kernels, call_place(): pl.pallas_call(functools.partial(place, z), out_shape=res, in_specs=[vmem...  4.77 us

profile of v3, /device:TPU:0, one launch (start us, length us, event | category | flops | bytes accessed | tf_op | source)
XLA Modules:
  0.0 209.6 jit_solution(5755630628486674724)
XLA Ops:
  1.3 203.4 %block.1 = (bf16[2,2,2,2,144,384]{5,4,3,2,1,0:T(8,128)(2,1)}, bf16[2,2,2,2,144,384]{5,4,3,2,1,0:T(8,128)(2,1)}, bf16[2,2,2,2,144,384]{5,4,3,2,1,0:T(8,128)(2,1)}...) custom-call(s32[1]{0:T(128)S(6)} %copy.33.refs_0_, ...), custom_call_target="tpu_custom_call" | custom-call | tf_op jit(solution)/shard_map/block/pallas_call | solution.py:1023
  204.7 4.8 %place.1 = (bf16[161,1152]{1,0:T(8,128)(2,1)}, bf16[161,1152]{1,0:T(8,128)(2,1)}, bf16[322,576]{1,0:T(8,128)(2,1)}, f32[72,1152]{1,0:T(8,128)}, f32[36]{0:T(128)...) custom-call(bf16[161,1152]{1,0:T(8,128)(2,1)} %get-tuple-element.41., ...), custom_call_target="tpu_custom_call" | custom-call | tf_op jit(solution)/shard_map/place/pallas_call | solution.py:1074
